TPU v7x, 512 devices: a whole 4x8x8 slice. The times are simulated.
512 devices in a mesh: dp: 32 (over x_hi, y, core), mp: 16 (over x_lo, z).
Axes of the slice: x: 4 (x_hi: 2, x_lo: 2; x = x_hi * 2 + x_lo), y: 8, z: 8, core: 2. Of those that a mesh axis runs over, the one named last changes fastest.
Arguments:
- tokens: bfloat16 [8192, 3072], P('dp'), may hold values from -6 to 6
- layer_norm_gain: float32 [3072], replicated, may hold values from 0.5 to 1.5
- w_up: bfloat16 [3072, 12288], P(None, 'mp'), may hold values from -0.109375 to 0.109375
- w_down: bfloat16 [12288, 3072], P('mp'), may hold values from -0.078125 to 0.078125
- cotangent: bfloat16 [8192, 3072], P(('dp', 'mp')), may hold values from -6 to 6
Outputs:
- mixed: bfloat16 [8192, 3072], P(('dp', 'mp'))
- grad_tokens: bfloat16 [8192, 3072], P(('dp', 'mp'))
- grad_up: bfloat16 [3072, 12288], P(None, 'mp')
- grad_down: bfloat16 [12288, 3072], P('mp')
- gradient_of_gain: float32 [3072], replicated
All inputs are finite; a program needn't handle non-finite values.
Results may differ from a plain program's by a relative error of at most 0.03.
Values may be sent and summed in bfloat16 or wider, within the bound.
A program may use at most 128 MiB of HBM per device.

v0:
```python
import math

import jax
import jax.numpy as jnp
from jax import lax
from jax.sharding import PartitionSpec as P


def apply_layer_norm(tokens):
    values = tokens.astype(jnp.float32)
    centred = values - jnp.mean(values, axis=1, keepdims=True)
    inverse_deviation = lax.rsqrt(jnp.mean(centred * centred, axis=1, keepdims=True) + 1e-06)
    return (centred * inverse_deviation, inverse_deviation)


def gelu_value(pre):
    return 0.5 * pre * (1.0 + jax.scipy.special.erf(pre / math.sqrt(2.0)))


def gelu_slope(pre):
    cumul = 0.5 * (1.0 + jax.scipy.special.erf(pre / math.sqrt(2.0)))
    density = jnp.exp(-0.5 * pre * pre) / math.sqrt(2.0 * math.pi)
    return cumul + pre * density


def contract_rows(left, right):
    return lax.dot_general(
        left, right, (((0,), (0,)), ((), ())), preferred_element_type=jnp.float32
    )


def contract_cols(left, right):
    return lax.dot_general(
        left, right, (((1,), (1,)), ((), ())), preferred_element_type=jnp.float32
    )


def shards(tokens, layer_norm_gain, w_up, w_down, cotangent):
    local_token_rows = cotangent.shape[0]
    leading_row_index = lax.axis_index("mp") * local_token_rows
    input_centred_hat, inverse_deviation = apply_layer_norm(tokens)
    normed_rows = (input_centred_hat * layer_norm_gain).astype(jnp.bfloat16)
    pre = jnp.dot(normed_rows, w_up, preferred_element_type=jnp.float32)
    act = gelu_value(pre).astype(jnp.bfloat16)
    piece = act
    branch = lax.psum_scatter(
        jnp.dot(piece, w_down, preferred_element_type=jnp.float32).astype(jnp.bfloat16),
        "mp",
        scatter_dimension=0,
        tiled=True,
    ).astype(jnp.float32)
    own_tokens = lax.dynamic_slice_in_dim(tokens, leading_row_index, local_token_rows, 0)
    mixed = (own_tokens.astype(jnp.float32) + branch).astype(jnp.bfloat16)
    cotangent_all = lax.all_gather(cotangent, "mp", axis=0, tiled=True)
    back_act = contract_cols(cotangent_all, w_down)
    down_part = contract_rows(act, cotangent_all)
    back_pre = (back_act * gelu_slope(pre)).astype(jnp.bfloat16)
    up_part = contract_rows(normed_rows, back_pre)
    grad_up, grad_down = (
        lax.psum(up_part.astype(jnp.bfloat16), "dp").astype(jnp.float32),
        lax.psum(down_part.astype(jnp.bfloat16), "dp").astype(jnp.float32),
    )
    piece = back_pre
    backward_normed_rows = lax.psum_scatter(
        contract_cols(piece, w_up).astype(jnp.bfloat16), "mp", scatter_dimension=0, tiled=True
    ).astype(jnp.float32)
    local_centred_hat = lax.dynamic_slice_in_dim(
        input_centred_hat, leading_row_index, local_token_rows, 0
    )
    own_inverse = lax.dynamic_slice_in_dim(
        inverse_deviation, leading_row_index, local_token_rows, 0
    )
    gain_part = jnp.sum(backward_normed_rows * local_centred_hat, axis=0)
    gradient_of_gain = lax.psum(gain_part, ("dp", "mp"))
    backward_centred_hat = backward_normed_rows * layer_norm_gain
    backward_input_rows = own_inverse * (
        backward_centred_hat
        - jnp.mean(backward_centred_hat, axis=1, keepdims=True)
        - local_centred_hat
        * jnp.mean(backward_centred_hat * local_centred_hat, axis=1, keepdims=True)
    )
    grad_tokens = (cotangent.astype(jnp.float32) + backward_input_rows).astype(jnp.bfloat16)
    return (
        mixed,
        grad_tokens,
        grad_up.astype(jnp.bfloat16),
        grad_down.astype(jnp.bfloat16),
        gradient_of_gain,
    )


def solution(mesh):
    placed = (P("dp", None), P(), P(None, "mp"), P("mp", None), P(("dp", "mp"), None))
    return jax.shard_map(
        shards,
        mesh=mesh,
        in_specs=placed,
        out_specs=(P(("dp", "mp"), None), P(("dp", "mp"), None), P(None, "mp"), P("mp", None), P()),
        check_vma=False,
    )
```

profile of v0, /device:TPU:1, one launch (start us, length us, event | category | flops | bytes accessed | tf_op | source)
XLA Modules:
  0.0 552.9 jit_solution(3647808750034129584)
XLA Ops:
  7.2 0.0 copy-start
  7.2 0.0 copy-start.5
  7.2 0.0 all-gather.2.cloned.1.call-start
  7.2 0.7 all-gather.2.cloned.1.call-update
  7.9 0.0 reduce-scatter.3.cloned.1.call-start
  8.0 1.7 convert_reduce_fusion
  9.7 0.0 slice-start.2
  9.7 2.1 fusion.2
  11.8 0.0 copy-done
  11.8 0.0 copy-done.5
  11.8 0.0 slice-start.3
  11.8 3.9 fusion.8
  15.7 0.0 slice-done.2
  15.7 0.0 slice-done.3
  15.7 0.0 copy-start.2
  15.8 2.6 convolution_convert_fusion.3
  18.4 0.0 reduce-scatter.3.cloned.1.call-update
  18.4 0.0 reduce-scatter.5.cloned.1.call-start
  18.5 61.6 %all-gather.2.cloned.1.call-done = bf16[256,3072]{1,0:T(8,128)(2,1)} async-done(((bf16[16,3072]{1,0:T(8,128)(2,1)}), bf16[256,3072]{1,0:T(8,128)(2,1)}) %all-gather.2.cloned.1.call-update) | async-done | bytes 1572880 | tf_op jit(solution)/shard_map/all_gather | solution.py:54
  80.1 0.0 copy-done.2
  80.1 4.4 fusion.3
  84.4 0.0 copy-start.6
  84.4 5.0 convolution_convert_fusion.2
  89.5 0.0 copy-done.6
  89.5 0.0 reduce-scatter.5.cloned.1.call-update
  89.5 0.0 copy-start.1
  89.5 0.0 all-reduce.3.cloned.1.call-start
  89.6 0.0 copy-start.3
  89.6 5.0 convolution_convert_fusion.1
  94.5 0.0 copy-done.1
  94.6 0.0 copy-done.3
  94.6 3.6 convolution_convert_fusion
  98.2 0.0 all-reduce.3.cloned.1.call-update
  98.2 0.0 copy-start.4
  98.2 0.1 dynamic-slice.3
  98.3 2.2 fusion
  100.5 54.1 %reduce-scatter.3.cloned.1.call-done = bf16[16,3072]{1,0:T(8,128)(2,1)} async-done(((bf16[256,3072]{1,0:T(8,128)(2,1)}), bf16[16,3072]{1,0:T(8,128)(2,1)}) %reduce-scatter.3.cloned.1.call-update) | async-done | bytes 98320 | tf_op jit(solution)/shard_map/reduce_scatter | solution.py:46
  154.6 1.6 add_convert_fusion
  156.2 73.5 %reduce-scatter.5.cloned.1.call-done = bf16[16,3072]{1,0:T(8,128)(2,1)} async-done(((bf16[256,3072]{1,0:T(8,128)(2,1)}), bf16[16,3072]{1,0:T(8,128)(2,1)}) %reduce-scatter.5.cloned.1.call-update) | async-done | bytes 98320 | tf_op jit(solution)/shard_map/reduce_scatter | solution.py:64
  229.7 1.2 fusion.17
  230.8 108.1 %psum.23 = f32[3072]{0:T(1024)} all-reduce(f32[3072]{0:T(1024)S(1)} %get-tuple-element.5), channel_id=1, replica_groups=mesh['dp'=32,'mp'=16] {'dp','mp'}, use_global_device_ids=true, to_apply=%region_9.0 | all-reduce | flops 3072 | bytes 24576 | tf_op jit(solution)/shard_map/psum | solution.py:74
  338.9 0.0 copy-done.4
  338.9 1.7 fusion.15
  340.7 198.5 %all-reduce.3.cloned.1.call-done = (bf16[3072,768]{1,0:T(8,128)(2,1)}, bf16[768,3072]{1,0:T(8,128)(2,1)}) async-done(((bf16[3072,768]{1,0:T(8,128)(2,1)}, bf16[768,3072]{1,0:T(8,128)(2,1)}), (bf16[3072,768]{1,0:T(8,128)(2,1)}, bf16[768,3072]{1,0:T(8,128)(2,1)})) %all-reduce.3.cloned.1.call-update) | async-done | bytes 9437200 | tf_op jit(solution)/shard_map/psum | solution.py:60
  539.2 5.0 copy.12
  544.1 0.0 slice-done
  544.1 0.0 slice-done.1
  544.2 2.2 copy.13
  (7 shorter events, 0.0 us)
Async XLA Ops:
  7.2 4.6 copy-start
  7.2 4.6 copy-start.5
  7.2 72.9 %all-gather.2.cloned.1.call-start = ((), (), s32[]{:S(2)}) async-start(), calls=%async_computation.3 | async-start | bytes 1671168 | tf_op jit(solution)/shard_map/all_gather | solution.py:54
  7.9 146.7 %reduce-scatter.3.cloned.1.call-start = ((), (), s32[]{:S(2)}) async-start(), calls=%async_computation.2 | async-start | bytes 1671168 | tf_op jit(solution)/shard_map/reduce_scatter | solution.py:46
  9.7 6.0 %slice-start.2 = ((s8[4718592]{0:T(1024)(128)(4,1)}), s8[4194304]{0:T(1024)(128)(4,1)S(1)}, s32[]{:S(2)}) async-start(s8[4718592]{0:T(1024)(128)(4,1)} %bitcast.10), calls=%async_computation.8 | async-start | bytes 8388608
  11.8 3.9 slice-start.3
  15.7 64.3 %copy-start.2 = (f32[256,768]{1,0:T(8,128)}, f32[256,768]{1,0:T(8,128)S(1)}, u32[]{:S(2)}) copy-start(f32[256,768]{1,0:T(8,128)S(1)} %fusion.8) | copy-start | bytes 2359300
  18.4 211.3 %reduce-scatter.5.cloned.1.call-start = ((), (), s32[]{:S(2)}) async-start(), calls=%async_computation.4 | async-start | bytes 1671168 | tf_op jit(solution)/shard_map/reduce_scatter | solution.py:64
  84.4 5.1 copy-start.6
  89.5 5.0 copy-start.1
  89.5 449.6 %all-reduce.3.cloned.1.call-start = ((), (), s32[]{:S(2)}) async-start(), calls=%async_computation.5 | async-start | bytes 18874368 | tf_op jit(solution)/shard_map/psum | solution.py:60
  89.6 5.0 copy-start.3
  98.2 240.7 %copy-start.4 = (bf16[16,3072]{1,0:T(8,128)(2,1)S(1)}, bf16[16,3072]{1,0:T(8,128)(2,1)}, u32[]{:S(2)}) copy-start(bf16[16,3072]{1,0:T(8,128)(2,1)} %param.9) | copy-start | bytes 294916
  539.2 5.0 slice-start
  539.2 5.0 slice-start.1
Sparse Core Ops, SparseCore 0:
  10.1 69.9 all-gather.1
  82.9 71.6 reduce-scatter.2
  157.7 71.9 reduce-scatter.4
  233.1 305.9 all-reduce.2
where the time goes:
time: 553 us
  waiting for transfers between devices  388 us (70%)
  blocking collectives  108 us (20%)
  matrix products  24.5 us (4%)
  between operations  13.9 us (3%)
  other arithmetic  10.5 us (2%)
  local copies, waits for them, and re-layouts  7.3 us (1%)
    psum x1, waiting for transfers between devices, shards(): lax.psum(up_part.astype(jnp.bfloat16), 'dp').astype(jnp.float32)  199 us
    psum x1, blocking collectives, shards(): gradient_of_gain = lax.psum(gain_part, ('dp', 'mp'))  108 us
    reduce_scatter x1, waiting for transfers between devices, shards(): lax.psum_scatter(contract_cols(piece, w_up).astype(jnp.bfloat16), 'mp', s...  73.5 us
    all_gather x1, waiting for transfers between devices, shards(): cotangent_all = lax.all_gather(cotangent, 'mp', axis=0, tiled=True)  61.6 us
    reduce_scatter x1, waiting for transfers between devices, shards(): lax.psum_scatter(jnp.dot(piece, w_down, preferred_element_type=jnp.float3...  54.1 us
  transfers between devices with their start and end apart: 4, of which 4 were waited for; matrix products, arithmetic and copies ran while one was open for 6% of the time, Pallas kernels for 0%

commit v1 on v0

v1 whole, which is shorter than its diff:
```python
import math

import jax
import jax.numpy as jnp
from jax import lax
from jax.experimental import pallas as pl
from jax.experimental.pallas import tpu as pltpu
from jax.sharding import PartitionSpec as P

F32 = jnp.float32
BF16 = jnp.bfloat16
D = 3072
HALF = D // 2
FF = 768
ROWS = 256
NY = 8
NZ = 8
OWN = 16
UC, UB, UA = 192, 48, 96
DC, DB, DA = 96, 384, 768
U, DN = 0, 1
GAIN_ROUNDS = 9


def gelu_value(pre):
    return 0.5 * pre * (1.0 + lax.erf(pre * (1.0 / math.sqrt(2.0))))


def gelu_slope(pre):
    cumul = 0.5 * (1.0 + lax.erf(pre * (1.0 / math.sqrt(2.0))))
    density = jnp.exp(-0.5 * pre * pre) * (1.0 / math.sqrt(2.0 * math.pi))
    return cumul + pre * density


def dot_nn(a, b):
    return lax.dot_general(a, b, (((1,), (0,)), ((), ())), preferred_element_type=F32)


def dot_nt(a, b):
    return lax.dot_general(a, b, (((1,), (1,)), ((), ())), preferred_element_type=F32)


def mod8(v):
    return lax.rem(v + 16, 8)


def flip(v, b):
    return v + b - 2 * b * lax.rem(v // b, 2)


def kernel(
    tok_hbm, gain, wu_hbm, wd_hbm, cot_hbm,
    mixed, gtok, gup_hbm, gdn_hbm, ggain,
    tok, wu, wd, nrm, mean, inv, nT, nTs, cot, cot_sib, act, slope, aT, bp, brp, bnp,
    zrecv, zx, gu, gd, ru, rd, xu, xd, xau, xad, fu, fd, gacc, grecv,
    lsem, csem, crsem, xlsem, exs, exr, rs_s, rs_r, xs_s, xs_r, xa_s, xa_r,
    z_s, z_r, zx_s, zx_r, ag_s, ag_r, sb_s, sb_r, fx_s, fx_r, sx_s, sx_r, gn_s, gn_r,
):
    dp = lax.axis_index("dp")
    mp = lax.axis_index("mp")
    c = lax.rem(dp, 2)
    y = lax.rem(dp // 2, NY)
    xh = dp // 16
    z = lax.rem(mp, NZ)
    xl = mp // NZ

    def at_y(v):
        return (xh * 16 + v * 2 + c, mp)

    def at_z(v):
        return (dp, xl * NZ + v)

    sib = (dp + 1 - 2 * c, mp)
    xpart = (xh * -16 + 16 + y * 2 + c, mp)
    lpart = (dp, (1 - xl) * NZ + z)
    ydev = [at_y(mod8(y + 1)), at_y(mod8(y - 1))]
    zdev = [at_z(mod8(z + 1)), at_z(mod8(z - 1))]
    sign = [1, -1]

    def remote(src, dst, ssem, rsem, to):
        return pltpu.make_async_remote_copy(
            src_ref=src, dst_ref=dst, send_sem=ssem, recv_sem=rsem,
            device_id=to, device_id_type=pl.DeviceIdType.MESH,
        )

    load_cot = pltpu.make_async_copy(cot_hbm, cot.at[pl.ds(mp * OWN, OWN)], lsem.at[0])
    load_tok = pltpu.make_async_copy(tok_hbm, tok, lsem.at[1])
    load_wu = pltpu.make_async_copy(wu_hbm, wu, lsem.at[2])
    load_wd = pltpu.make_async_copy(wd_hbm, wd, lsem.at[3])
    for one in (load_cot, load_tok, load_wu, load_wd):
        one.start()
    barrier = pltpu.get_barrier_semaphore()
    greet = ydev + zdev + [
        sib, xpart, lpart, at_z(flip(z, 2)), at_z(flip(z, 4)), at_y(flip(y, 2)), at_y(flip(y, 4)),
    ]
    for one in greet:
        pl.semaphore_signal(barrier, inc=1, device_id=one, device_id_type=pl.DeviceIdType.MESH)
    pl.semaphore_wait(barrier, len(greet))

    def cot_rows(q, k):
        side = xl if q == 0 else 1 - xl
        return pl.ds(pl.multiple_of((side * NZ + k) * OWN, OWN), OWN)

    def cot_copy(q, j, d):
        rows = cot_rows(q, mod8(z - sign[d] * (j - 1)))
        ref = cot.at[rows] if j < 4 else cot.at[rows, pl.ds(d * HALF, HALF)]
        return remote(ref, ref, csem.at[q, j - 1, d], crsem.at[q, j - 1, d], zdev[d])

    def cot_arrival(q, j, d):
        rows = cot_rows(q, mod8(z - sign[d] * j))
        ref = cot.at[rows] if j < 4 else cot.at[rows, pl.ds(d * HALF, HALF)]
        return remote(ref, ref, csem.at[q, j - 1, d], crsem.at[q, j - 1, d], zdev[d])

    def cot_send(q, j):
        for d in range(2):
            cot_copy(q, j, d).start()

    def cot_wait(q, j):
        for d in range(2):
            cot_arrival(q, j, d).wait_recv()

    mine = cot.at[cot_rows(0, z)]
    theirs = cot.at[cot_rows(1, z)]
    load_cot.wait()
    cot_to_l = remote(mine, mine, xlsem.at[0], xlsem.at[1], lpart)
    cot_to_l.start()
    cot_send(0, 1)

    load_tok.wait()

    @pl.loop(0, ROWS // 32)
    def _(i):
        rows = pl.ds(pl.multiple_of(i * 32, 32), 32)
        v = tok[rows, :].astype(F32)
        mu = jnp.mean(v, axis=1, keepdims=True)
        cen = v - mu
        iv = lax.rsqrt(jnp.mean(cen * cen, axis=1, keepdims=True) + 1e-06)
        mean[rows, :] = mu
        inv[rows, :] = iv
        nrm[rows, :] = (cen * iv * gain[...]).astype(BF16)

    remote(theirs, theirs, xlsem.at[0], xlsem.at[1], lpart).wait_recv()
    cot_send(1, 1)
    cot_wait(0, 1)
    cot_send(0, 2)

    load_wu.wait()

    def pre_tile(t):
        cols = pl.ds(t * 256, 256)
        pre = dot_nn(nrm[...], wu[:, cols])
        a = gelu_value(pre)
        act[:, cols] = a.astype(BF16)
        slope[:, cols] = gelu_slope(pre)
        aT[cols, pl.ds(0, ROWS)] = a.T.astype(BF16)

    pre_tile(0)
    cot_wait(1, 1)
    cot_send(1, 2)
    cot_wait(0, 2)
    cot_send(0, 3)
    pre_tile(1)
    cot_wait(1, 2)
    cot_send(1, 3)
    cot_wait(0, 3)
    cot_send(0, 4)
    pre_tile(2)
    cot_wait(1, 3)
    cot_send(1, 4)

    mineK, theirsK = pl.ds(0, ROWS), pl.ds(ROWS, ROWS)
    act_x = remote(aT.at[:, mineK], aT.at[:, theirsK], exs.at[0], exr.at[0], sib)
    act_x.start()

    @pl.loop(0, HALF // 256)
    def _(j):
        rows = pl.ds(pl.multiple_of(j * 256, 256), 256)
        own = pl.ds(pl.multiple_of(c * HALF + j * 256, 256), 256)
        other = pl.ds(pl.multiple_of((1 - c) * HALF + j * 256, 256), 256)
        nT[rows, mineK] = nrm[:, own].astype(F32).T.astype(BF16)
        nTs[rows, :] = nrm[:, other].astype(F32).T.astype(BF16)

    nrm_x = remote(nTs, nT.at[:, theirsK], exs.at[1], exr.at[1], sib)
    nrm_x.start()

    load_wd.wait()

    @pl.loop(0, D // 512)
    def _(t):
        cols = pl.ds(pl.multiple_of(t * 512, 512), 512)
        brp[:, :, :, cols] = dot_nn(act[...], wd[:, cols]).astype(BF16).reshape(2, NZ, OWN, 512)

    for q in range(2):
        cot_wait(q, 4)

    ownC = pl.ds(pl.multiple_of(c * HALF, HALF), HALF)
    otherC = pl.ds(pl.multiple_of((1 - c) * HALF, HALF), HALF)
    cot_x = remote(cot.at[:, otherC], cot_sib, exs.at[2], exr.at[2], sib)
    cot_x.start()

    @pl.loop(0, FF // 256)
    def _(t):
        rows = pl.ds(pl.multiple_of(t * 256, 256), 256)
        back = dot_nt(cot[...], wd[rows, :])
        bp[mineK, rows] = (back * slope[:, rows]).astype(BF16)

    bp_x = remote(bp.at[mineK], bp.at[theirsK], exs.at[3], exr.at[3], sib)
    bp_x.start()

    def reg(kind, k, d, lo, n, base):
        if kind == U:
            return (pl.ds(pl.multiple_of(base + k * UC + lo, 16), n), pl.ds(d * 384, 384))
        return (pl.ds(pl.multiple_of(k * DC + d * 48, 16), 48), pl.ds(pl.multiple_of(base + lo, 128), n))

    unit = (UB, DB)
    ring_n = (UA + UB, DA + DB)

    def ring(kind, k, d, base=0):
        return reg(kind, k, d, xh * unit[kind], ring_n[kind], base)

    def part_a(kind, k, d, base=0):
        return reg(kind, k, d, unit[kind], 2 * unit[kind], base)

    def part_b(kind, k, d, side, base=0):
        return reg(kind, k, d, side * 3 * unit[kind], unit[kind], base)

    g = (gu, gd)
    rr = (ru, rd)
    xr = (xu, xd)
    xa = (xau, xad)
    f = (fu, fd)

    def rs_chunk(s, d):
        return mod8(y - sign[d] * (1 + s))

    def x_first(kind, s, d):
        k = rs_chunk(s, d)
        return remote(
            g[kind].at[part_b(kind, k, d, 1 - xh)], xr[kind].at[s, d],
            xs_s.at[kind, s, d], xs_r.at[kind, s, d], xpart,
        )

    def x_first_all(kind):
        @pl.loop(0, NY)
        def _(s):
            for d in range(2):
                x_first(kind, s, d).start()

    remote(aT.at[:, mineK], aT.at[:, theirsK], exs.at[0], exr.at[0], sib).wait_recv()
    remote(cot.at[:, otherC], cot_sib, exs.at[2], exr.at[2], sib).wait_recv()

    @pl.loop(0, HALF // 512)
    def _(t):
        cols = pl.ds(pl.multiple_of(t * 512, 512), 512)
        part = pl.ds(pl.multiple_of(c * HALF + t * 512, 512), 512)
        gd[:, cols] = (
            dot_nn(aT[:, mineK], cot[:, part]) + dot_nn(aT[:, theirsK], cot_sib[:, cols])
        ).astype(BF16)

    x_first_all(DN)

    remote(nTs, nT.at[:, theirsK], exs.at[1], exr.at[1], sib).wait_recv()
    remote(bp.at[mineK], bp.at[theirsK], exs.at[3], exr.at[3], sib).wait_recv()

    @pl.loop(0, HALF // 512)
    def _(t):
        rows = pl.ds(pl.multiple_of(t * 512, 512), 512)
        gu[rows, :] = dot_nn(nT[rows, :], bp[...]).astype(BF16)

    x_first_all(U)

    def rs_copy(kind, s, d):
        k = rs_chunk(s, d)
        return remote(
            g[kind].at[ring(kind, k, d)], rr[kind].at[s, d], rs_s.at[kind, s, d], rs_r.at[kind, s, d], ydev[d],
        )

    def rs_step(s, first, last):
        for kind in (DN, U):
            for d in range(2):
                k = rs_chunk(s, d)
                x_first(kind, s, d).wait_recv()
                b = part_b(kind, k, d, xh)
                g[kind][b] = (g[kind][b].astype(F32) + xr[kind][s, d].astype(F32)).astype(BF16)
                if not first:
                    rs_copy(kind, s - 1, d).wait_recv()
                    r = ring(kind, k, d)
                    g[kind][r] = (g[kind][r].astype(F32) + rr[kind][s - 1, d].astype(F32)).astype(BF16)
                if not last:
                    rs_copy(kind, s, d).start()

    zp = (brp, bnp)

    def z_copy(kind, s, d):
        k = mod8(z - sign[d] * (1 + s))
        return remote(
            zp[kind].at[:, k, :, pl.ds(d * HALF, HALF)], zrecv.at[kind, s, d],
            z_s.at[kind, s, d], z_r.at[kind, s, d], zdev[d],
        )

    def z_step(s, first, last):
        for kind in range(2):
            for d in range(2):
                if not first:
                    z_copy(kind, s - 1, d).wait_recv()
                    k = mod8(z - sign[d] * (1 + s))
                    cols = pl.ds(d * HALF, HALF)
                    zp[kind][:, k, :, cols] = (
                        zp[kind][:, k, :, cols].astype(F32) + zrecv[kind, s - 1, d].astype(F32)
                    ).astype(BF16)
                if not last:
                    z_copy(kind, s, d).start()

    def gain_copy(r):
        to_dp, to_mp = dp, mp
        for n, (a, b) in enumerate(
            [
                at_z(flip(z, 1)), at_z(flip(z, 2)), at_z(flip(z, 4)),
                at_y(flip(y, 1)), at_y(flip(y, 2)), at_y(flip(y, 4)),
                lpart, xpart, sib,
            ]
        ):
            to_dp = jnp.where(r == n, a, to_dp)
            to_mp = jnp.where(r == n, b, to_mp)
        return remote(gacc.at[r], grecv.at[r], gn_s.at[r], gn_r.at[r], (to_dp, to_mp))

    def gain_finish(r):
        gain_copy(r).wait_recv()
        gacc[r + 1] = gacc[r] + grecv[r]

    rs_step(0, True, False)

    @pl.loop(0, D // 512)
    def _(t):
        cols = pl.ds(pl.multiple_of(t * 512, 512), 512)
        back = dot_nt(bp[mineK, :], wu[cols, :])
        bnp[:, :, :, cols] = back.astype(BF16).reshape(2, NZ, OWN, 512)
        hat = (tok[:, cols].astype(F32) - mean[...]) * inv[...]
        gacc[0, :, cols] = jnp.sum(back * hat, axis=0, keepdims=True)

    z_step(0, True, False)
    gain_copy(0).start()

    @pl.loop(1, 7)
    def _(s):
        rs_step(s, False, False)
        z_step(s, False, False)
        gain_finish(s - 1)
        gain_copy(s).start()

    rs_step(7, False, True)

    def a_copy(kind, d):
        return remote(
            g[kind].at[part_a(kind, y, d)], xa[kind].at[d], xa_s.at[kind, d], xa_r.at[kind, d], xpart,
        )

    for kind in (DN, U):
        for d in range(2):
            a_copy(kind, d).start()

    z_step(7, False, True)

    def zx_copy(kind):
        return remote(zp[kind].at[1 - xl, z], zx.at[kind], zx_s.at[kind], zx_r.at[kind], lpart)

    for kind in range(2):
        zx_copy(kind).start()
    gain_finish(6)
    gain_copy(7).start()

    def base(core):
        return core * HALF

    def ag_chunk(s, d):
        return mod8(y - sign[d] * s)

    def same(kind, r, ssem, rsem, to):
        return remote(f[kind].at[r], f[kind].at[r], ssem, rsem, to)

    def ag_copy(kind, s, d):
        return same(kind, ring(kind, ag_chunk(s, d), d, base(c)), ag_s.at[kind, s, d], ag_r.at[kind, s, d], ydev[d])

    def ag_arrival(kind, s, d):
        return same(kind, ring(kind, ag_chunk(s, d), d, base(c)), ag_s.at[kind, s - 1, d], ag_r.at[kind, s - 1, d], ydev[d])

    def sib_copy(kind, s, d, core):
        return same(kind, ring(kind, ag_chunk(s, d), d, base(core)), sb_s.at[kind, s, d], sb_r.at[kind, s, d], sib)

    def fx_copy(kind, s, d, side):
        return same(kind, part_b(kind, ag_chunk(s, d), d, side, base(c)), fx_s.at[kind, s, d], fx_r.at[kind, s, d], xpart)

    def sx_copy(kind, s, d, core):
        return same(kind, part_b(kind, ag_chunk(s, d), d, 1 - xh, base(core)), sx_s.at[kind, s, d], sx_r.at[kind, s, d], sib)

    for kind in (DN, U):
        for d in range(2):
            a_copy(kind, d).wait_recv()
            b, b_f = part_b(kind, y, d, xh), part_b(kind, y, d, xh, base(c))
            f[kind][b_f] = g[kind][b]
            a, a_f = part_a(kind, y, d), part_a(kind, y, d, base(c))
            f[kind][a_f] = (g[kind][a].astype(F32) + xa[kind][d].astype(F32)).astype(BF16)
            ag_copy(kind, 0, d).start()
            fx_copy(kind, 0, d, xh).start()
            sib_copy(kind, 0, d, c).start()

    rows = pl.ds(pl.multiple_of(mp * OWN, OWN), OWN)
    own_tok = tok[rows, :].astype(F32)
    for kind in range(2):
        zx_copy(kind).wait_recv()
    mixed[...] = (own_tok + (brp[xl, z].astype(F32) + zx[0].astype(F32))).astype(BF16)
    back_normed = bnp[xl, z].astype(F32) + zx[1].astype(F32)
    hat = (own_tok - mean[rows, :]) * inv[rows, :]
    back_hat = back_normed * gain[...]
    back_in = inv[rows, :] * (
        back_hat
        - jnp.mean(back_hat, axis=1, keepdims=True)
        - hat * jnp.mean(back_hat * hat, axis=1, keepdims=True)
    )
    gtok[...] = (cot[rows, :].astype(F32) + back_in).astype(BF16)

    def ag_step(s, last):
        for kind in (DN, U):
            for d in range(2):
                ag_arrival(kind, s, d).wait_recv()
                if not last:
                    ag_copy(kind, s, d).start()
                fx_copy(kind, s, d, xh).start()
                sib_copy(kind, s, d, c).start()
        for kind in (DN, U):
            for d in range(2):
                fx_copy(kind, s - 1, d, 1 - xh).wait_recv()
                sx_copy(kind, s - 1, d, c).start()

    @pl.loop(1, 7)
    def _(s):
        ag_step(s, False)

        @pl.when(s == 1)
        def _():
            gain_finish(7)
            gain_copy(8).start()

        @pl.when(s == 2)
        def _():
            gain_finish(8)

    ag_step(7, True)
    ggain[...] = gacc[GAIN_ROUNDS]
    for kind in (DN, U):
        for d in range(2):
            fx_copy(kind, 7, d, 1 - xh).wait_recv()
            sx_copy(kind, 7, d, c).start()

    @pl.loop(0, NY)
    def _(s):
        for kind in (DN, U):
            for d in range(2):
                sib_copy(kind, s, d, 1 - c).wait_recv()
                sx_copy(kind, s, d, 1 - c).wait_recv()

    out_u = pltpu.make_async_copy(fu, gup_hbm, lsem.at[4])
    out_d = pltpu.make_async_copy(fd, gdn_hbm, lsem.at[5])
    out_u.start()
    out_d.start()

    cot_to_l.wait_send()
    for q in range(2):
        for j in range(1, 5):
            for d in range(2):
                cot_copy(q, j, d).wait_send()
    for one in (act_x, nrm_x, cot_x, bp_x):
        one.wait_send()

    @pl.loop(0, NY)
    def _(s):
        for kind in range(2):
            for d in range(2):
                x_first(kind, s, d).wait_send()
                fx_copy(kind, s, d, xh).wait_send()
                sib_copy(kind, s, d, c).wait_send()
                sx_copy(kind, s, d, c).wait_send()

    @pl.loop(0, NY - 1)
    def _(s):
        for kind in range(2):
            for d in range(2):
                rs_copy(kind, s, d).wait_send()
                ag_copy(kind, s, d).wait_send()
                z_copy(kind, s, d).wait_send()

    for kind in range(2):
        zx_copy(kind).wait_send()
        for d in range(2):
            a_copy(kind, d).wait_send()

    @pl.loop(0, GAIN_ROUNDS)
    def _(r):
        gain_copy(r).wait_send()

    out_u.wait()
    out_d.wait()


def shards(tokens, layer_norm_gain, w_up, w_down, cotangent):
    anywhere = pl.BlockSpec(memory_space=pl.ANY)
    vmem = pl.BlockSpec(memory_space=pltpu.VMEM)
    dma = pltpu.SemaphoreType.DMA
    both = (2, NY, 2)
    mixed, grad_tokens, grad_up, grad_down, gain_grad = pl.pallas_call(
        kernel,
        out_shape=(
            jax.ShapeDtypeStruct((OWN, D), BF16),
            jax.ShapeDtypeStruct((OWN, D), BF16),
            jax.ShapeDtypeStruct((D, FF), BF16),
            jax.ShapeDtypeStruct((FF, D), BF16),
            jax.ShapeDtypeStruct((1, D), F32),
        ),
        in_specs=[anywhere, vmem, anywhere, anywhere, anywhere],
        out_specs=(vmem, vmem, anywhere, anywhere, vmem),
        scratch_shapes=[
            pltpu.VMEM((ROWS, D), BF16),
            pltpu.VMEM((D, FF), BF16),
            pltpu.VMEM((FF, D), BF16),
            pltpu.VMEM((ROWS, D), BF16),
            pltpu.VMEM((ROWS, 1), F32),
            pltpu.VMEM((ROWS, 1), F32),
            pltpu.VMEM((HALF, 2 * ROWS), BF16),
            pltpu.VMEM((HALF, ROWS), BF16),
            pltpu.VMEM((ROWS, D), BF16),
            pltpu.VMEM((ROWS, HALF), BF16),
            pltpu.VMEM((ROWS, FF), BF16),
            pltpu.VMEM((ROWS, FF), F32),
            pltpu.VMEM((FF, 2 * ROWS), BF16),
            pltpu.VMEM((2 * ROWS, FF), BF16),
            pltpu.VMEM((2, NZ, OWN, D), BF16),
            pltpu.VMEM((2, NZ, OWN, D), BF16),
            pltpu.VMEM((2, NZ - 1, 2, 2, OWN, HALF), BF16),
            pltpu.VMEM((2, OWN, D), BF16),
            pltpu.VMEM((HALF, FF), BF16),
            pltpu.VMEM((FF, HALF), BF16),
            pltpu.VMEM((NY - 1, 2, UA + UB, 384), BF16),
            pltpu.VMEM((NY - 1, 2, 48, DA + DB), BF16),
            pltpu.VMEM((NY, 2, UB, 384), BF16),
            pltpu.VMEM((NY, 2, 48, DB), BF16),
            pltpu.VMEM((2, UA, 384), BF16),
            pltpu.VMEM((2, 48, DA), BF16),
            pltpu.VMEM((D, FF), BF16),
            pltpu.VMEM((FF, D), BF16),
            pltpu.VMEM((GAIN_ROUNDS + 1, 1, D), F32),
            pltpu.VMEM((GAIN_ROUNDS, 1, D), F32),
            dma((6,)),
            dma((2, 4, 2)), dma((2, 4, 2)), dma((2,)),
            dma((4,)), dma((4,)),
            dma(both), dma(both), dma(both), dma(both),
            dma((2, 2)), dma((2, 2)),
            dma(both), dma(both), dma((2,)), dma((2,)),
            dma(both), dma(both), dma(both), dma(both),
            dma(both), dma(both), dma(both), dma(both),
            dma((GAIN_ROUNDS,)), dma((GAIN_ROUNDS,)),
        ],
        compiler_params=pltpu.CompilerParams(
            collective_id=0, has_side_effects=True, vmem_limit_bytes=58 * 2**20
        ),
        cost_estimate=pl.CostEstimate(
            flops=12 * ROWS * D * FF, bytes_accessed=22 * 2**20, transcendentals=2 * ROWS * FF
        ),
        name="mlp_block",
    )(tokens, layer_norm_gain.reshape(1, D), w_up, w_down, cotangent)
    return mixed, grad_tokens, grad_up, grad_down, gain_grad.reshape(D)


def solution(mesh):
    placed = (P("dp", None), P(), P(None, "mp"), P("mp", None), P(("dp", "mp"), None))
    return jax.shard_map(
        shards,
        mesh=mesh,
        in_specs=placed,
        out_specs=(P(("dp", "mp"), None), P(("dp", "mp"), None), P(None, "mp"), P("mp", None), P()),
        check_vma=False,
    )
```

time: 553 us -> 165 us (0.30)
  waiting for transfers between devices: 388 us -> 0 us
  Pallas kernels: 0 us -> 154 us
  blocking collectives: 108 us -> 0 us
  matrix products: 24.5 us -> 0 us
  between operations: 13.9 us -> 0.65 us
  other arithmetic: 10.5 us -> 0.01 us
    psum x1 -> x0, waiting for transfers between devices: 199 us -> none  [shards(): lax.psum(up_part.astype(jnp.bfloat16), 'dp').astype(jnp.float32)]
    pallas_call x0 -> x1, Pallas kernels: none -> 154 us  [shards(): pl.pallas_call(kernel, out_shape=(jax.ShapeDtypeStruct((OWN, D), BF16), j...]
    reduce_scatter x2 -> x0, waiting for transfers between devices: 128 us -> none  [the longest x1 73.5 us: shards(): lax.psum_scatter(contract_cols(piece, w_up).astype(jnp.bfloat16), 'mp', s...]
    psum x1 -> x0, blocking collectives: 108 us -> none  [shards(): gradient_of_gain = lax.psum(gain_part, ('dp', 'mp'))]
    all_gather x1 -> x0, waiting for transfers between devices: 61.6 us -> none  [shards(): cotangent_all = lax.all_gather(cotangent, 'mp', axis=0, tiled=True)]
    dot_general x6 -> x0, matrix products: 24.5 us -> none  [the longest x2 9.4 us: contract_cols(): lax.dot_general(left, right, (((1,), (1,)), ((), ())), preferred_element_...]
  transfers between devices with their start and end apart: 4 -> 0, of which waited for: 4 -> 0; matrix products, arithmetic and copies ran while one was open for 6% -> 0% of each run, Pallas kernels for 0% -> 0%
where the time goes in v1:
time: 165 us
  Pallas kernels  154 us (93%)
  local copies, waits for them, and re-layouts  10.9 us (7%)
    pallas_call x1, Pallas kernels, shards(): pl.pallas_call(kernel, out_shape=(jax.ShapeDtypeStruct((OWN, D), BF16), j...  154 us
    unnamed x11, local copies, waits for them, and re-layouts  10.9 us

profile of v1, /device:TPU:1, one launch (start us, length us, event | category | flops | bytes accessed | tf_op | source)
XLA Modules:
  0.0 165.2 jit_solution(1109562674002571236)
XLA Ops:
  0.6 153.6 %mlp_block.1 = (bf16[16,3072]{1,0:T(8,128)(2,1)}, bf16[16,3072]{1,0:T(8,128)(2,1)}, bf16[3072,768]{1,0:T(8,128)(2,1)}, bf16[768,3072]{1,0:T(8,128)(2,1)}, f32[1,3072]{1,0:T(1,128)}) custom-call(bf16[256,3072]{1,0:T(8,128)(2,1)} %tok_hbm.1, f32[1,3072]{1,0:T(1,128)} %bitcast.5, bf16[3072,768]{1,0:T(8,128)(2,1)} %wu_hbm.1, bf16[768,3072]{1,0:T(8,128)(2,1)} %wd_hbm.1, ...), custom_call_target="tpu_custom_call" | custom-call | flops 7247757312 | bytes 23068672 | tf_op jit(solution)/shard_map/mlp_block/pallas_call | solution.py:510
  154.3 1.5 copy.15
  155.8 0.0 slice-start
  155.8 1.7 %copy.16 = bf16[16,3072]{1,0:T(8,128)(2,1)} copy(bf16[16,3072]{1,0:T(8,128)(2,1)} %get-tuple-element.21) | data formatting | bytes 196608
  157.5 0.0 slice-start.1
  157.5 4.9 %copy.17 = bf16[3072,768]{1,0:T(8,128)(2,1)} copy(bf16[3072,768]{1,0:T(8,128)(2,1)} %get-tuple-element.22) | data formatting | bytes 9437184
  162.4 0.0 slice-done
  162.4 0.0 slice-done.1
  162.4 0.0 copy-start
  162.4 2.2 %copy.18 = bf16[768,3072]{1,0:T(8,128)(2,1)} copy(bf16[768,3072]{1,0:T(8,128)(2,1)S(1)} %bitcast.3) | data formatting | bytes 9437184
  164.6 0.0 copy-done
  164.6 0.6 copy.19
  (1 shorter events, 0.0 us)
Async XLA Ops:
  155.8 6.6 %slice-start = ((s8[4718592]{0:T(1024)(128)(4,1)}), s8[4194304]{0:T(1024)(128)(4,1)S(1)}, s32[]{:S(2)}) async-start(s8[4718592]{0:T(1024)(128)(4,1)} %bitcast.2), calls=%async_computation | async-start | bytes 8388608
  157.5 4.9 %slice-start.1 = ((s8[4718592]{0:T(1024)(128)(4,1)}), s8[524288]{0:T(1024)(128)(4,1)S(1)}, s32[]{:S(2)}) async-start(s8[4718592]{0:T(1024)(128)(4,1)} %bitcast.2), calls=%async_computation.1 | async-start | bytes 1048576
  162.4 2.2 %copy-start = (f32[1,3072]{1,0:T(1,128)S(1)}, f32[1,3072]{1,0:T(1,128)}, u32[]{:S(2)}) copy-start(f32[1,3072]{1,0:T(1,128)} %get-tuple-element.14) | copy-start | bytes 36868

commit v2 on v1

v2 whole, which is shorter than its diff:
```python
import math

import jax
import jax.numpy as jnp
from jax import lax
from jax.experimental import pallas as pl
from jax.experimental.pallas import tpu as pltpu
from jax.sharding import PartitionSpec as P

F32 = jnp.float32
BF16 = jnp.bfloat16
D = 3072
HALF = D // 2
FF = 768
ROWS = 256
NY = 8
NZ = 8
OWN = 16
UC, DC = 192, 96
UR, UW = 48, 384
U, DN = 0, 1
GAIN_ROUNDS = 6


def gelu_value(pre):
    return 0.5 * pre * (1.0 + lax.erf(pre * (1.0 / math.sqrt(2.0))))


def gelu_slope(pre):
    cumul = 0.5 * (1.0 + lax.erf(pre * (1.0 / math.sqrt(2.0))))
    density = jnp.exp(-0.5 * pre * pre) * (1.0 / math.sqrt(2.0 * math.pi))
    return cumul + pre * density


def dot_nn(a, b):
    return lax.dot_general(a, b, (((1,), (0,)), ((), ())), preferred_element_type=F32)


def dot_nt(a, b):
    return lax.dot_general(a, b, (((1,), (1,)), ((), ())), preferred_element_type=F32)


def mod8(v):
    return lax.rem(v + 16, 8)


def flip(v, b):
    return v + b - 2 * b * lax.rem(v // b, 2)


def kernel(
    tok_hbm, gain, wu_hbm, wd_hbm, cot_hbm,
    mixed, gtok, fu, fd, ggain,
    tok, wu, wd, nrm, mean, inv, nT, nTs, cot, cot_sib, act, slope, aT, bp, brp, bnp,
    zrecv, zx, gu, gd, rr, xr, xa, gz, gacc, grecv,
    lsem, sent, crsem, exr, rs_r, xs_r, xa_r, z_r, zx_r, ag_r, sib_r, fx_r, gz_r, gn_r,
):
    dp = lax.axis_index("dp")
    mp = lax.axis_index("mp")
    c = lax.rem(dp, 2)
    y = lax.rem(dp // 2, NY)
    xh = dp // 16
    z = lax.rem(mp, NZ)
    xl = mp // NZ

    s_cot, s_ex, s_rs, s_x1, s_xa, s_z, s_zx, s_ag, s_sib, s_fx, s_gz, s_gn = (sent.at[i] for i in range(12))

    def at_y(v):
        return (xh * 16 + v * 2 + c, mp)

    def at_z(v):
        return (dp, xl * NZ + v)

    sib = (dp + 1 - 2 * c, mp)
    xpart = (xh * -16 + 16 + y * 2 + c, mp)
    lpart = (dp, (1 - xl) * NZ + z)
    ydev = [at_y(mod8(y + 1)), at_y(mod8(y - 1))]
    zdev = [at_z(mod8(z + 1)), at_z(mod8(z - 1))]
    sign = [1, -1]

    def remote(src, dst, ssem, rsem, to):
        return pltpu.make_async_remote_copy(
            src_ref=src, dst_ref=dst, send_sem=ssem, recv_sem=rsem,
            device_id=to, device_id_type=pl.DeviceIdType.MESH,
        )

    load_cot = pltpu.make_async_copy(cot_hbm, cot.at[pl.ds(mp * OWN, OWN)], lsem.at[0])
    load_tok = pltpu.make_async_copy(tok_hbm, tok, lsem.at[1])
    load_wu = pltpu.make_async_copy(wu_hbm, wu, lsem.at[2])
    load_wd = pltpu.make_async_copy(wd_hbm, wd, lsem.at[3])
    for one in (load_cot, load_tok, load_wu, load_wd):
        one.start()
    barrier = pltpu.get_barrier_semaphore()
    zall = [at_z(mod8(z + j)) for j in range(1, NZ)]
    greet = ydev + zall + [sib, xpart, lpart, at_y(flip(y, 2)), at_y(flip(y, 4))]
    for one in greet:
        pl.semaphore_signal(barrier, inc=1, device_id=one, device_id_type=pl.DeviceIdType.MESH)
    pl.semaphore_wait(barrier, len(greet))

    def cot_rows(q, k):
        side = xl if q == 0 else 1 - xl
        return pl.ds(pl.multiple_of((side * NZ + k) * OWN, OWN), OWN)

    def cot_copy(q, j, d):
        rows = cot_rows(q, mod8(z - sign[d] * (j - 1)))
        ref = cot.at[rows] if j < 4 else cot.at[rows, pl.ds(d * HALF, HALF)]
        return remote(ref, ref, s_cot, crsem.at[q, j - 1, d], zdev[d])

    def cot_arrival(q, j, d):
        rows = cot_rows(q, mod8(z - sign[d] * j))
        ref = cot.at[rows] if j < 4 else cot.at[rows, pl.ds(d * HALF, HALF)]
        return remote(ref, ref, s_cot, crsem.at[q, j - 1, d], zdev[d])

    def cot_send(q, j):
        for d in range(2):
            cot_copy(q, j, d).start()

    def cot_wait(q, j):
        for d in range(2):
            cot_arrival(q, j, d).wait_recv()

    mine = cot.at[cot_rows(0, z)]
    theirs = cot.at[cot_rows(1, z)]
    load_cot.wait()
    cot_to_l = remote(mine, mine, s_cot, crsem.at[0, 4, 0], lpart)
    cot_to_l.start()
    cot_send(0, 1)

    load_tok.wait()

    def layer_norm(lo, hi):
        @pl.loop(lo // 32, hi // 32)
        def _(i):
            rows = pl.ds(pl.multiple_of(i * 32, 32), 32)
            v = tok[rows, :].astype(F32)
            mu = jnp.mean(v, axis=1, keepdims=True)
            cen = v - mu
            iv = lax.rsqrt(jnp.mean(cen * cen, axis=1, keepdims=True) + 1e-06)
            mean[rows, :] = mu
            inv[rows, :] = iv
            nrm[rows, :] = (cen * iv * gain[...]).astype(BF16)

    layer_norm(0, 128)
    remote(theirs, theirs, s_cot, crsem.at[0, 4, 0], lpart).wait_recv()
    cot_send(1, 1)
    layer_norm(128, 256)
    cot_wait(0, 1)
    cot_send(0, 2)

    load_wu.wait()

    def pre_tile(t):
        cols = pl.ds(t * 256, 256)
        pre = dot_nn(nrm[...], wu[:, cols])
        a = gelu_value(pre)
        act[:, cols] = a.astype(BF16)
        slope[:, cols] = gelu_slope(pre)
        aT[cols, pl.ds(0, ROWS)] = a.T.astype(BF16)

    mineK, theirsK = pl.ds(0, ROWS), pl.ds(ROWS, ROWS)
    act_x = remote(aT.at[:, mineK], aT.at[:, theirsK], s_ex, exr.at[0], sib)

    pre_tile(0)
    cot_wait(1, 1)
    cot_send(1, 2)
    pre_tile(1)
    cot_wait(0, 2)
    cot_send(0, 3)
    pre_tile(2)
    act_x.start()
    cot_wait(1, 2)
    cot_send(1, 3)

    @pl.loop(0, HALF // 256)
    def _(j):
        rows = pl.ds(pl.multiple_of(j * 256, 256), 256)
        own = pl.ds(pl.multiple_of(c * HALF + j * 256, 256), 256)
        other = pl.ds(pl.multiple_of((1 - c) * HALF + j * 256, 256), 256)
        nT[rows, mineK] = nrm[:, own].astype(F32).T.astype(BF16)
        nTs[rows, :] = nrm[:, other].astype(F32).T.astype(BF16)

    nrm_x = remote(nTs, nT.at[:, theirsK], s_ex, exr.at[1], sib)
    nrm_x.start()

    load_wd.wait()
    cot_wait(0, 3)
    cot_send(0, 4)

    @pl.loop(0, D // 512)
    def _(t):
        cols = pl.ds(pl.multiple_of(t * 512, 512), 512)
        brp[:, :, :, cols] = dot_nn(act[...], wd[:, cols]).astype(BF16).reshape(2, NZ, OWN, 512)

    cot_wait(1, 3)
    cot_send(1, 4)
    for q in range(2):
        cot_wait(q, 4)

    ownC = pl.ds(pl.multiple_of(c * HALF, HALF), HALF)
    otherC = pl.ds(pl.multiple_of((1 - c) * HALF, HALF), HALF)
    cot_x = remote(cot.at[:, otherC], cot_sib, s_ex, exr.at[2], sib)
    cot_x.start()

    zp = (brp, bnp)

    def z_cols(s, d):
        return (slice(None), mod8(z - sign[d] * (1 + s)), slice(None), pl.ds(d * HALF, HALF))

    def z_copy(kind, s, d):
        return remote(
            zp[kind].at[z_cols(s, d)], zrecv.at[kind, s, d], s_z, z_r.at[kind, s, d], zdev[d],
        )

    def z_step(kind, s, first=False, last=False):
        for d in range(2):
            if not first:
                z_copy(kind, s - 1, d).wait_recv()
                zp[kind][z_cols(s, d)] = (
                    zp[kind][z_cols(s, d)].astype(F32) + zrecv[kind, s - 1, d].astype(F32)
                ).astype(BF16)
            if not last:
                z_copy(kind, s, d).start()

    def zx_copy(kind):
        return remote(zp[kind].at[1 - xl, z], zx.at[kind], s_zx, zx_r.at[kind], lpart)

    z_step(0, 0, first=True)

    @pl.loop(0, FF // 256)
    def _(t):
        rows = pl.ds(pl.multiple_of(t * 256, 256), 256)
        back = dot_nt(cot[...], wd[rows, :])
        bp[mineK, rows] = (back * slope[:, rows]).astype(BF16)

    bp_x = remote(bp.at[mineK], bp.at[theirsK], s_ex, exr.at[3], sib)
    bp_x.start()
    z_step(0, 1)

    def unit(kind, k, d, u, n=1, base=0):
        if kind == U:
            return (pl.ds(pl.multiple_of(base + k * UC + u * UR, 16), n * UR), pl.ds(d * UW, UW))
        return (pl.ds(pl.multiple_of(k * DC + d * UR, 16), UR), pl.ds(pl.multiple_of(base + u * UW, 128), n * UW))

    g = (gu, gd)
    f = (fu, fd)
    kinds = (DN, U)
    mine_u = (1, 2, 3 * xh)

    def rs_chunk(s, d):
        return mod8(y - sign[d] * (1 + s))

    def x_first(kind, s, d):
        return remote(
            g[kind].at[unit(kind, rs_chunk(s, d), d, 3 - 3 * xh)], xr.at[kind, s, d],
            s_x1, xs_r.at[kind, s, d], xpart,
        )

    def x_first_start(kind, s):
        for d in range(2):
            x_first(kind, s, d).start()

    remote(aT.at[:, mineK], aT.at[:, theirsK], s_ex, exr.at[0], sib).wait_recv()
    remote(cot.at[:, otherC], cot_sib, s_ex, exr.at[2], sib).wait_recv()

    @pl.loop(0, HALF // 512)
    def _(t):
        cols = pl.ds(pl.multiple_of(t * 512, 512), 512)
        part = pl.ds(pl.multiple_of(c * HALF + t * 512, 512), 512)
        gd[:, cols] = (
            dot_nn(aT[:, mineK], cot[:, part]) + dot_nn(aT[:, theirsK], cot_sib[:, cols])
        ).astype(BF16)

    x_first_start(DN, 0)
    x_first_start(DN, 1)
    z_step(0, 2)

    remote(nTs, nT.at[:, theirsK], s_ex, exr.at[1], sib).wait_recv()
    remote(bp.at[mineK], bp.at[theirsK], s_ex, exr.at[3], sib).wait_recv()

    @pl.loop(0, HALF // 512)
    def _(t):
        rows = pl.ds(pl.multiple_of(t * 512, 512), 512)
        gu[rows, :] = dot_nn(nT[rows, :], bp[...]).astype(BF16)

    x_first_start(U, 0)
    x_first_start(U, 1)
    z_step(0, 3)

    def rs_copy(kind, s, d, p):
        return remote(
            g[kind].at[unit(kind, rs_chunk(s, d), d, mine_u[p])], rr.at[kind, s, d, p],
            s_rs, rs_r.at[kind, s, d, p], ydev[d],
        )

    def rs_step(kind, s, first=False, last=False):
        for p in range(3):
            for d in range(2):
                at = unit(kind, rs_chunk(s, d), d, mine_u[p])
                if p == 2:
                    x_first(kind, s, d).wait_recv()
                if not first:
                    rs_copy(kind, s - 1, d, p).wait_recv()
                if p == 2 or not first:
                    total = g[kind][at].astype(F32)
                    if p == 2:
                        total = total + xr[kind, s, d].astype(F32)
                    if not first:
                        total = total + rr[kind, s - 1, d, p].astype(F32)
                    g[kind][at] = total.astype(BF16)
                if not last:
                    rs_copy(kind, s, d, p).start()

    partners = [at_y(flip(y, 1)), at_y(flip(y, 2)), at_y(flip(y, 4)), lpart, xpart, sib]

    def gz_copy(j):
        return remote(gz.at[z], gz.at[z], s_gz, gz_r.at[0], zall[j - 1])

    def gain_copy(r):
        return remote(gacc.at[r], grecv.at[r], s_gn, gn_r.at[r], partners[r])

    def gain_z_finish():
        seven = gz.at[pl.ds(0, NZ - 1)]
        remote(seven, seven, s_gz, gz_r.at[0], sib).wait_recv()
        total = gz[0]
        for k in range(1, NZ):
            total = total + gz[k]
        gacc[0] = total
        gain_copy(0).start()

    def gain_finish(r):
        gain_copy(r).wait_recv()
        gacc[r + 1] = gacc[r] + grecv[r]
        if r + 1 < GAIN_ROUNDS:
            gain_copy(r + 1).start()

    rs_step(DN, 0, first=True)
    x_first_start(DN, 2)

    @pl.loop(0, D // 512)
    def _(t):
        cols = pl.ds(pl.multiple_of(t * 512, 512), 512)
        back = dot_nt(bp[mineK, :], wu[cols, :])
        bnp[:, :, :, cols] = back.astype(BF16).reshape(2, NZ, OWN, 512)
        hat = (tok[:, cols].astype(F32) - mean[...]) * inv[...]
        gz[z, :, cols] = jnp.sum(back * hat, axis=0, keepdims=True)

    rs_step(U, 0, first=True)
    x_first_start(U, 2)
    z_step(0, 4)
    z_step(1, 0, first=True)
    for j in range(1, NZ):
        gz_copy(j).start()

    @pl.loop(1, 7)
    def _(s):
        for kind in kinds:
            rs_step(kind, s)

            @pl.when(s < 6)
            def _():
                x_first_start(kind, s + 2)

        @pl.when(s < 3)
        def _():
            z_step(0, s + 4)

        @pl.when(s == 3)
        def _():
            z_step(0, 7, last=True)
            zx_copy(0).start()

        @pl.when(s > 3)
        def _():
            z_step(1, s - 3)

        @pl.when(s == 3)
        def _():
            gain_z_finish()

        @pl.when(s == 5)
        def _():
            gain_finish(0)

    def a_copy(kind, d, p):
        return remote(
            g[kind].at[unit(kind, y, d, mine_u[p])], xa.at[kind, d, p], s_xa, xa_r.at[kind, d, p], xpart,
        )

    def ag_chunk(s, d):
        return mod8(y - sign[d] * s)

    def same(kind, at, ssem, rsem, to):
        return remote(f[kind].at[at], f[kind].at[at], ssem, rsem, to)

    def out_unit(kind, s, d, u, n=1, core=c):
        return unit(kind, ag_chunk(s, d), d, u, n, core * HALF)

    def ag_copy(kind, s, d, p):
        return same(kind, out_unit(kind, s, d, mine_u[p]), s_ag, ag_r.at[kind, s, d, p], ydev[d])

    def ag_arrival(kind, s, d, p):
        return same(kind, out_unit(kind, s, d, mine_u[p]), s_ag, ag_r.at[kind, s - 1, d, p], ydev[d])

    def sa_copy(kind, s, d, core=c):
        return same(kind, out_unit(kind, s, d, 1, 2, core), s_sib, sib_r.at[0], sib)

    def sb_copy(kind, s, d, core=c):
        return same(kind, out_unit(kind, s, d, 3 * xh, 1, core), s_sib, sib_r.at[0], sib)

    def fx_copy(kind, s, d, side=xh):
        return same(kind, out_unit(kind, s, d, 3 * side), s_fx, fx_r.at[kind, s, d], xpart)

    def sx_copy(kind, s, d, core=c):
        return same(kind, out_unit(kind, s, d, 3 - 3 * xh, 1, core), s_sib, sib_r.at[0], sib)

    def x_arrived(s):
        for kind in kinds:
            for d in range(2):
                fx_copy(kind, s, d, 1 - xh).wait_recv()
                sx_copy(kind, s, d).start()

    def ag_a(s, send=True):
        for kind in kinds:
            for p in range(2):
                for d in range(2):
                    ag_arrival(kind, s, d, p).wait_recv()
                    if send:
                        ag_copy(kind, s, d, p).start()
        for kind in kinds:
            for d in range(2):
                sa_copy(kind, s, d).start()

    def ag_b(s, send=True):
        for kind in kinds:
            for d in range(2):
                ag_arrival(kind, s, d, 2).wait_recv()
                if send:
                    ag_copy(kind, s, d, 2).start()
                fx_copy(kind, s, d).start()
        for kind in kinds:
            for d in range(2):
                sb_copy(kind, s, d).start()

    for kind in kinds:
        rs_step(kind, 7, last=True)
        for p in range(2):
            for d in range(2):
                a_copy(kind, d, p).start()
        for d in range(2):
            f[kind][out_unit(kind, 0, d, 3 * xh)] = g[kind][unit(kind, y, d, 3 * xh)]
            ag_copy(kind, 0, d, 2).start()
            fx_copy(kind, 0, d).start()
            sb_copy(kind, 0, d).start()
    gain_finish(1)
    z_step(1, 4)
    ag_b(1)
    for kind in kinds:
        for p in range(2):
            for d in range(2):
                a_copy(kind, d, p).wait_recv()
                f[kind][out_unit(kind, 0, d, mine_u[p])] = (
                    g[kind][unit(kind, y, d, mine_u[p])].astype(F32) + xa[kind, d, p].astype(F32)
                ).astype(BF16)
                ag_copy(kind, 0, d, p).start()
        for d in range(2):
            sa_copy(kind, 0, d).start()
    ag_b(2)

    @pl.loop(1, NY)
    def _(s):
        @pl.when(s < 7)
        def _():
            ag_a(s)

        @pl.when(s == 7)
        def _():
            ag_a(7, False)

        @pl.when(s < 5)
        def _():
            ag_b(s + 2)

        @pl.when(s == 5)
        def _():
            ag_b(7, False)

        x_arrived(s - 1)

        @pl.when(s < 3)
        def _():
            z_step(1, s + 4)

        @pl.when(s == 3)
        def _():
            z_step(1, 7, last=True)
            zx_copy(1).start()

        @pl.when(s == 2)
        def _():
            gain_finish(2)

        @pl.when(s == 4)
        def _():
            gain_finish(3)

        @pl.when(s == 6)
        def _():
            gain_finish(4)

    x_arrived(7)

    rows = pl.ds(pl.multiple_of(mp * OWN, OWN), OWN)
    own_tok = tok[rows, :].astype(F32)
    zx_copy(0).wait_recv()
    mixed[...] = (own_tok + (brp[xl, z].astype(F32) + zx[0].astype(F32))).astype(BF16)
    zx_copy(1).wait_recv()
    back_normed = bnp[xl, z].astype(F32) + zx[1].astype(F32)
    hat = (own_tok - mean[rows, :]) * inv[rows, :]
    back_hat = back_normed * gain[...]
    back_in = inv[rows, :] * (
        back_hat
        - jnp.mean(back_hat, axis=1, keepdims=True)
        - hat * jnp.mean(back_hat * hat, axis=1, keepdims=True)
    )
    gtok[...] = (cot[rows, :].astype(F32) + back_in).astype(BF16)
    gain_finish(5)
    ggain[...] = gacc[GAIN_ROUNDS]

    remote(fu, fu, s_sib, sib_r.at[0], sib).wait_recv()

    def all_sent(sem, ref):
        remote(ref, ref, sem, sib_r.at[0], sib).wait_send()

    all_sent(s_cot, cot.at[pl.ds(0, ROWS - OWN)])
    all_sent(s_ex, gu)
    all_sent(s_rs, rr)
    all_sent(s_x1, xr)
    all_sent(s_xa, xa)
    all_sent(s_z, zrecv)
    all_sent(s_zx, zx)
    all_sent(s_ag, rr)
    all_sent(s_sib, fu)
    all_sent(s_fx, xr)
    all_sent(s_gz, gz.at[pl.ds(0, NZ - 1)])
    all_sent(s_gn, gacc.at[pl.ds(0, GAIN_ROUNDS)])


def shards(tokens, layer_norm_gain, w_up, w_down, cotangent):
    anywhere = pl.BlockSpec(memory_space=pl.ANY)
    vmem = pl.BlockSpec(memory_space=pltpu.VMEM)
    dma = pltpu.SemaphoreType.DMA
    shapes = [((OWN, D), BF16), ((OWN, D), BF16), ((D, FF), BF16), ((FF, D), BF16), ((1, D), F32)]
    mixed, grad_tokens, grad_up, grad_down, gain_grad = pl.pallas_call(
        kernel,
        out_shape=tuple(pltpu.VMEM(shape, dtype) for shape, dtype in shapes),
        in_specs=[anywhere, vmem, anywhere, anywhere, anywhere],
        out_specs=(vmem,) * 5,
        scratch_shapes=[
            pltpu.VMEM((ROWS, D), BF16),
            pltpu.VMEM((D, FF), BF16),
            pltpu.VMEM((FF, D), BF16),
            pltpu.VMEM((ROWS, D), BF16),
            pltpu.VMEM((ROWS, 1), F32),
            pltpu.VMEM((ROWS, 1), F32),
            pltpu.VMEM((HALF, 2 * ROWS), BF16),
            pltpu.VMEM((HALF, ROWS), BF16),
            pltpu.VMEM((ROWS, D), BF16),
            pltpu.VMEM((ROWS, HALF), BF16),
            pltpu.VMEM((ROWS, FF), BF16),
            pltpu.VMEM((ROWS, FF), F32),
            pltpu.VMEM((FF, 2 * ROWS), BF16),
            pltpu.VMEM((2 * ROWS, FF), BF16),
            pltpu.VMEM((2, NZ, OWN, D), BF16),
            pltpu.VMEM((2, NZ, OWN, D), BF16),
            pltpu.VMEM((2, NZ - 1, 2, 2, OWN, HALF), BF16),
            pltpu.VMEM((2, OWN, D), BF16),
            pltpu.VMEM((HALF, FF), BF16),
            pltpu.VMEM((FF, HALF), BF16),
            pltpu.VMEM((2, NY - 1, 2, 3, UR, UW), BF16),
            pltpu.VMEM((2, NY, 2, UR, UW), BF16),
            pltpu.VMEM((2, 2, 2, UR, UW), BF16),
            pltpu.VMEM((NZ, 1, D), F32),
            pltpu.VMEM((GAIN_ROUNDS + 1, 1, D), F32),
            pltpu.VMEM((GAIN_ROUNDS, 1, D), F32),
            dma((4,)), dma((12,)),
            dma((2, 5, 2)), dma((4,)),
            dma((2, NY - 1, 2, 3)), dma((2, NY, 2)), dma((2, 2, 2)),
            dma((2, NZ - 1, 2)), dma((2,)),
            dma((2, NY - 1, 2, 3)), dma((1,)), dma((2, NY, 2)),
            dma((1,)), dma((GAIN_ROUNDS,)),
        ],
        compiler_params=pltpu.CompilerParams(
            collective_id=0, has_side_effects=True, vmem_limit_bytes=46 * 2**20
        ),
        cost_estimate=pl.CostEstimate(
            flops=12 * ROWS * D * FF, bytes_accessed=22 * 2**20, transcendentals=2 * ROWS * FF
        ),
        name="mlp_block",
    )(tokens, layer_norm_gain.reshape(1, D), w_up, w_down, cotangent)
    return mixed, grad_tokens, grad_up, grad_down, gain_grad.reshape(D)


def solution(mesh):
    placed = (P("dp", None), P(), P(None, "mp"), P("mp", None), P(("dp", "mp"), None))
    return jax.shard_map(
        shards,
        mesh=mesh,
        in_specs=placed,
        out_specs=(P(("dp", "mp"), None), P(("dp", "mp"), None), P(None, "mp"), P("mp", None), P()),
        check_vma=False,
    )
```

time: 165 us -> 134 us (0.81)
  Pallas kernels: 154 us -> 127 us
  local copies, waits for them, and re-layouts: 10.9 us -> 6.25 us
    pallas_call x1, Pallas kernels: 154 us -> 127 us  [shards(): pl.pallas_call(kernel, out_shape=tuple((pltpu.VMEM(shape, dtype) for shap...]
    unnamed x11 -> x5, local copies, waits for them, and re-layouts: 10.9 us -> 6.25 us
where the time goes in v2:
time: 134 us
  Pallas kernels  127 us (95%)
  local copies, waits for them, and re-layouts  6.25 us (5%)
    pallas_call x1, Pallas kernels, shards(): pl.pallas_call(kernel, out_shape=tuple((pltpu.VMEM(shape, dtype) for shap...  127 us
    unnamed x5, local copies, waits for them, and re-layouts  6.25 us

profile of v2, /device:TPU:1, one launch (start us, length us, event | category | flops | bytes accessed | tf_op | source)
XLA Modules:
  0.0 133.6 jit_solution(9403449225437600622)
XLA Ops:
  0.6 126.7 %mlp_block.1 = (bf16[16,3072]{1,0:T(8,128)(2,1)S(1)}, bf16[16,3072]{1,0:T(8,128)(2,1)S(1)}, bf16[3072,768]{1,0:T(8,128)(2,1)S(1)}, bf16[768,3072]{1,0:T(8,128)(2,1)S(1)}, f32[1,3072]{1,0:T(1,128)S(1)}) custom-call(bf16[256,3072]{1,0:T(8,128)(2,1)} %tok_hbm.1, f32[1,3072]{1,0:T(1,128)} %bitcast.3, bf16[3072,768]{1,0:T(8,128)(2,1)} %wu_hbm.1, ...), custom_call_target="tpu_custom_call" | custom-call | flops 7247757312 | bytes 23068672 | tf_op jit(solution)/shard_map/mlp_block/pallas_call | solution.py:553
  127.3 0.6 copy.15
  127.9 0.6 copy.19
  128.5 0.6 copy.16
  129.2 2.2 %copy.17 = bf16[3072,768]{1,0:T(8,128)(2,1)} copy(bf16[3072,768]{1,0:T(8,128)(2,1)S(1)} %get-tuple-element.17) | data formatting | bytes 9437184
  131.4 2.2 %copy.18 = bf16[768,3072]{1,0:T(8,128)(2,1)} copy(bf16[768,3072]{1,0:T(8,128)(2,1)S(1)} %get-tuple-element.18) | data formatting | bytes 9437184

commit v3 on v2

--- a/solution.py
+++ b/solution.py
@@ -38,6 +38,11 @@
 
 def dot_nt(a, b):
     return lax.dot_general(a, b, (((1,), (1,)), ((), ())), preferred_element_type=F32)
+
+
+def flat(*at):
+    place = (at[0] * NY + at[1]) * 2 + at[2]
+    return place if len(at) == 3 else place * 3 + at[3]
 
 
 def mod8(v):
@@ -97,34 +102,33 @@
         pl.semaphore_signal(barrier, inc=1, device_id=one, device_id_type=pl.DeviceIdType.MESH)
     pl.semaphore_wait(barrier, len(greet))
 
-    def cot_rows(q, k):
-        side = xl if q == 0 else 1 - xl
-        return pl.ds(pl.multiple_of((side * NZ + k) * OWN, OWN), OWN)
-
-    def cot_copy(q, j, d):
-        rows = cot_rows(q, mod8(z - sign[d] * (j - 1)))
-        ref = cot.at[rows] if j < 4 else cot.at[rows, pl.ds(d * HALF, HALF)]
-        return remote(ref, ref, s_cot, crsem.at[q, j - 1, d], zdev[d])
-
-    def cot_arrival(q, j, d):
-        rows = cot_rows(q, mod8(z - sign[d] * j))
-        ref = cot.at[rows] if j < 4 else cot.at[rows, pl.ds(d * HALF, HALF)]
-        return remote(ref, ref, s_cot, crsem.at[q, j - 1, d], zdev[d])
-
-    def cot_send(q, j):
+    def cot_half(k, h):
+        return (pl.ds(pl.multiple_of((xl * NZ + k) * OWN, OWN), OWN), pl.ds(h * HALF, HALF))
+
+    def cot_ring(k, j, d, h):
+        ref = cot.at[cot_half(k, h)]
+        return remote(ref, ref, s_cot, crsem.at[(j - 1) * 4 + d * 2 + h], zdev[d])
+
+    def cot_send(j, d, h):
+        cot_ring(mod8(z - sign[d] * (j - 1)), j, d, h).start()
+
+    def cot_next(j, h):
         for d in range(2):
-            cot_copy(q, j, d).start()
-
-    def cot_wait(q, j):
+            if j == 4 and d != h:
+                continue
+            k = mod8(z - sign[d] * j)
+            cot_ring(k, j, d, h).wait_recv()
+            if j < 3 or (j == 3 and d == h):
+                cot_send(j + 1, d, h)
+            ref = cot.at[cot_half(k, h)]
+            remote(ref, ref, s_cot, crsem.at[14], lpart).start()
+
+    load_cot.wait()
+    for h in range(2):
         for d in range(2):
-            cot_arrival(q, j, d).wait_recv()
-
-    mine = cot.at[cot_rows(0, z)]
-    theirs = cot.at[cot_rows(1, z)]
-    load_cot.wait()
-    cot_to_l = remote(mine, mine, s_cot, crsem.at[0, 4, 0], lpart)
-    cot_to_l.start()
-    cot_send(0, 1)
+            cot_send(1, d, h)
+    mine = cot.at[pl.ds(pl.multiple_of(mp * OWN, OWN), OWN)]
+    remote(mine, mine, s_cot, crsem.at[14], lpart).start()
 
     load_tok.wait()
 
@@ -140,12 +144,9 @@
             inv[rows, :] = iv
             nrm[rows, :] = (cen * iv * gain[...]).astype(BF16)
 
-    layer_norm(0, 128)
-    remote(theirs, theirs, s_cot, crsem.at[0, 4, 0], lpart).wait_recv()
-    cot_send(1, 1)
-    layer_norm(128, 256)
-    cot_wait(0, 1)
-    cot_send(0, 2)
+    layer_norm(0, ROWS)
+    cot_next(1, 0)
+    cot_next(1, 1)
 
     load_wu.wait()
 
@@ -161,15 +162,15 @@
     act_x = remote(aT.at[:, mineK], aT.at[:, theirsK], s_ex, exr.at[0], sib)
 
     pre_tile(0)
-    cot_wait(1, 1)
-    cot_send(1, 2)
+    cot_next(2, 0)
+    cot_next(2, 1)
     pre_tile(1)
-    cot_wait(0, 2)
-    cot_send(0, 3)
+    cot_next(3, 0)
+    cot_next(3, 1)
     pre_tile(2)
     act_x.start()
-    cot_wait(1, 2)
-    cot_send(1, 3)
+    cot_next(4, 0)
+    cot_next(4, 1)
 
     @pl.loop(0, HALF // 256)
     def _(j):
@@ -183,18 +184,14 @@
     nrm_x.start()
 
     load_wd.wait()
-    cot_wait(0, 3)
-    cot_send(0, 4)
 
     @pl.loop(0, D // 512)
     def _(t):
         cols = pl.ds(pl.multiple_of(t * 512, 512), 512)
         brp[:, :, :, cols] = dot_nn(act[...], wd[:, cols]).astype(BF16).reshape(2, NZ, OWN, 512)
 
-    cot_wait(1, 3)
-    cot_send(1, 4)
-    for q in range(2):
-        cot_wait(q, 4)
+    eight = cot.at[pl.ds(0, NZ * OWN)]
+    remote(eight, eight, s_cot, crsem.at[14], lpart).wait_recv()
 
     ownC = pl.ds(pl.multiple_of(c * HALF, HALF), HALF)
     otherC = pl.ds(pl.multiple_of((1 - c) * HALF, HALF), HALF)
@@ -208,7 +205,7 @@
 
     def z_copy(kind, s, d):
         return remote(
-            zp[kind].at[z_cols(s, d)], zrecv.at[kind, s, d], s_z, z_r.at[kind, s, d], zdev[d],
+            zp[kind].at[z_cols(s, d)], zrecv.at[kind, s, d], s_z, z_r.at[flat(kind, s, d)], zdev[d],
         )
 
     def z_step(kind, s, first=False, last=False):
@@ -234,7 +231,6 @@
 
     bp_x = remote(bp.at[mineK], bp.at[theirsK], s_ex, exr.at[3], sib)
     bp_x.start()
-    z_step(0, 1)
 
     def unit(kind, k, d, u, n=1, base=0):
         if kind == U:
@@ -252,48 +248,21 @@
     def x_first(kind, s, d):
         return remote(
             g[kind].at[unit(kind, rs_chunk(s, d), d, 3 - 3 * xh)], xr.at[kind, s, d],
-            s_x1, xs_r.at[kind, s, d], xpart,
+            s_x1, xs_r.at[flat(kind, s, d)], xpart,
         )
 
     def x_first_start(kind, s):
         for d in range(2):
             x_first(kind, s, d).start()
 
-    remote(aT.at[:, mineK], aT.at[:, theirsK], s_ex, exr.at[0], sib).wait_recv()
-    remote(cot.at[:, otherC], cot_sib, s_ex, exr.at[2], sib).wait_recv()
-
-    @pl.loop(0, HALF // 512)
-    def _(t):
-        cols = pl.ds(pl.multiple_of(t * 512, 512), 512)
-        part = pl.ds(pl.multiple_of(c * HALF + t * 512, 512), 512)
-        gd[:, cols] = (
-            dot_nn(aT[:, mineK], cot[:, part]) + dot_nn(aT[:, theirsK], cot_sib[:, cols])
-        ).astype(BF16)
-
-    x_first_start(DN, 0)
-    x_first_start(DN, 1)
-    z_step(0, 2)
-
-    remote(nTs, nT.at[:, theirsK], s_ex, exr.at[1], sib).wait_recv()
-    remote(bp.at[mineK], bp.at[theirsK], s_ex, exr.at[3], sib).wait_recv()
-
-    @pl.loop(0, HALF // 512)
-    def _(t):
-        rows = pl.ds(pl.multiple_of(t * 512, 512), 512)
-        gu[rows, :] = dot_nn(nT[rows, :], bp[...]).astype(BF16)
-
-    x_first_start(U, 0)
-    x_first_start(U, 1)
-    z_step(0, 3)
-
     def rs_copy(kind, s, d, p):
         return remote(
             g[kind].at[unit(kind, rs_chunk(s, d), d, mine_u[p])], rr.at[kind, s, d, p],
-            s_rs, rs_r.at[kind, s, d, p], ydev[d],
+            s_rs, rs_r.at[flat(kind, s, d, p)], ydev[d],
         )
 
-    def rs_step(kind, s, first=False, last=False):
-        for p in range(3):
+    def rs_step(kind, s, pieces=(0, 1, 2), first=False, last=False):
+        for p in pieces:
             for d in range(2):
                 at = unit(kind, rs_chunk(s, d), d, mine_u[p])
                 if p == 2:
@@ -310,6 +279,35 @@
                 if not last:
                     rs_copy(kind, s, d, p).start()
 
+    remote(aT.at[:, mineK], aT.at[:, theirsK], s_ex, exr.at[0], sib).wait_recv()
+    remote(cot.at[:, otherC], cot_sib, s_ex, exr.at[2], sib).wait_recv()
+
+    @pl.loop(0, HALF // 512)
+    def _(t):
+        cols = pl.ds(pl.multiple_of(t * 512, 512), 512)
+        part = pl.ds(pl.multiple_of(c * HALF + t * 512, 512), 512)
+        gd[:, cols] = (
+            dot_nn(aT[:, mineK], cot[:, part]) + dot_nn(aT[:, theirsK], cot_sib[:, cols])
+        ).astype(BF16)
+
+    x_first_start(DN, 0)
+    rs_step(DN, 0, (0, 1), first=True)
+    x_first_start(DN, 1)
+
+    remote(nTs, nT.at[:, theirsK], s_ex, exr.at[1], sib).wait_recv()
+    remote(bp.at[mineK], bp.at[theirsK], s_ex, exr.at[3], sib).wait_recv()
+
+    @pl.loop(0, HALF // 512)
+    def _(t):
+        rows = pl.ds(pl.multiple_of(t * 512, 512), 512)
+        gu[rows, :] = dot_nn(nT[rows, :], bp[...]).astype(BF16)
+
+    x_first_start(U, 0)
+    rs_step(U, 0, (0, 1), first=True)
+    x_first_start(U, 1)
+    z_step(0, 1)
+
+
     partners = [at_y(flip(y, 1)), at_y(flip(y, 2)), at_y(flip(y, 4)), lpart, xpart, sib]
 
     def gz_copy(j):
@@ -333,7 +331,7 @@
         if r + 1 < GAIN_ROUNDS:
             gain_copy(r + 1).start()
 
-    rs_step(DN, 0, first=True)
+    rs_step(DN, 0, (2,), first=True)
     x_first_start(DN, 2)
 
     @pl.loop(0, D // 512)
@@ -344,10 +342,9 @@
         hat = (tok[:, cols].astype(F32) - mean[...]) * inv[...]
         gz[z, :, cols] = jnp.sum(back * hat, axis=0, keepdims=True)
 
-    rs_step(U, 0, first=True)
+    rs_step(U, 0, (2,), first=True)
     x_first_start(U, 2)
-    z_step(0, 4)
-    z_step(1, 0, first=True)
+    z_step(0, 2)
     for j in range(1, NZ):
         gz_copy(j).start()
 
@@ -360,15 +357,19 @@
             def _():
                 x_first_start(kind, s + 2)
 
-        @pl.when(s < 3)
-        def _():
-            z_step(0, s + 4)
-
-        @pl.when(s == 3)
+        @pl.when(s < 5)
+        def _():
+            z_step(0, s + 2)
+
+        @pl.when(s == 5)
         def _():
             z_step(0, 7, last=True)
             zx_copy(0).start()
 
+        @pl.when(s == 3)
+        def _():
+            z_step(1, 0, first=True)
+
         @pl.when(s > 3)
         def _():
             z_step(1, s - 3)
@@ -383,40 +384,54 @@
 
     def a_copy(kind, d, p):
         return remote(
-            g[kind].at[unit(kind, y, d, mine_u[p])], xa.at[kind, d, p], s_xa, xa_r.at[kind, d, p], xpart,
+            g[kind].at[unit(kind, y, d, mine_u[p])], xa.at[kind, d, p], s_xa, xa_r.at[kind * 4 + d * 2 + p], xpart,
         )
 
     def ag_chunk(s, d):
         return mod8(y - sign[d] * s)
 
-    def same(kind, at, ssem, rsem, to):
-        return remote(f[kind].at[at], f[kind].at[at], ssem, rsem, to)
-
-    def out_unit(kind, s, d, u, n=1, core=c):
-        return unit(kind, ag_chunk(s, d), d, u, n, core * HALF)
+    def out_unit(kind, s, d, u, n=1):
+        return unit(kind, ag_chunk(s, d), d, u, n, c * HALF)
+
+    def own(kind, d, p):
+        return xa.at[kind, d, p] if p < 2 else g[kind].at[unit(kind, y, d, 3 * xh)]
+
+    def out_copy(kind, s, d, p, ssem, rsem, to):
+        dst = f[kind].at[out_unit(kind, s, d, mine_u[p])]
+        return remote(own(kind, d, p) if isinstance(s, int) and s == 0 else dst, dst, ssem, rsem, to)
 
     def ag_copy(kind, s, d, p):
-        return same(kind, out_unit(kind, s, d, mine_u[p]), s_ag, ag_r.at[kind, s, d, p], ydev[d])
+        return out_copy(kind, s, d, p, s_ag, ag_r.at[flat(kind, s, d, p)], ydev[d])
 
     def ag_arrival(kind, s, d, p):
-        return same(kind, out_unit(kind, s, d, mine_u[p]), s_ag, ag_r.at[kind, s - 1, d, p], ydev[d])
-
-    def sa_copy(kind, s, d, core=c):
-        return same(kind, out_unit(kind, s, d, 1, 2, core), s_sib, sib_r.at[0], sib)
-
-    def sb_copy(kind, s, d, core=c):
-        return same(kind, out_unit(kind, s, d, 3 * xh, 1, core), s_sib, sib_r.at[0], sib)
-
-    def fx_copy(kind, s, d, side=xh):
-        return same(kind, out_unit(kind, s, d, 3 * side), s_fx, fx_r.at[kind, s, d], xpart)
-
-    def sx_copy(kind, s, d, core=c):
-        return same(kind, out_unit(kind, s, d, 3 - 3 * xh, 1, core), s_sib, sib_r.at[0], sib)
+        at = f[kind].at[out_unit(kind, s, d, mine_u[p])]
+        return remote(at, at, s_ag, ag_r.at[flat(kind, s - 1, d, p)], ydev[d])
+
+    def sib_copy(kind, s, d, p):
+        return out_copy(kind, s, d, p, s_sib, sib_r.at[0], sib)
+
+    def sa_copy(kind, s, d):
+        at = f[kind].at[out_unit(kind, s, d, 1, 2)]
+        return remote(at, at, s_sib, sib_r.at[0], sib)
+
+    def fx_copy(kind, s, d):
+        return out_copy(kind, s, d, 2, s_fx, fx_r.at[flat(kind, s, d)], xpart)
+
+    def keep(kind, d, p):
+        return pltpu.make_async_copy(own(kind, d, p), f[kind].at[out_unit(kind, 0, d, mine_u[p])], lsem.at[4])
+
+    def fx_arrival(kind, s, d):
+        at = f[kind].at[out_unit(kind, s, d, 3 - 3 * xh)]
+        return remote(at, at, s_fx, fx_r.at[flat(kind, s, d)], xpart)
+
+    def sx_copy(kind, s, d):
+        at = f[kind].at[out_unit(kind, s, d, 3 - 3 * xh)]
+        return remote(at, at, s_sib, sib_r.at[0], sib)
 
     def x_arrived(s):
         for kind in kinds:
             for d in range(2):
-                fx_copy(kind, s, d, 1 - xh).wait_recv()
+                fx_arrival(kind, s, d).wait_recv()
                 sx_copy(kind, s, d).start()
 
     def ag_a(s, send=True):
@@ -439,7 +454,7 @@
                 fx_copy(kind, s, d).start()
         for kind in kinds:
             for d in range(2):
-                sb_copy(kind, s, d).start()
+                sib_copy(kind, s, d, 2).start()
 
     for kind in kinds:
         rs_step(kind, 7, last=True)
@@ -447,10 +462,10 @@
             for d in range(2):
                 a_copy(kind, d, p).start()
         for d in range(2):
-            f[kind][out_unit(kind, 0, d, 3 * xh)] = g[kind][unit(kind, y, d, 3 * xh)]
             ag_copy(kind, 0, d, 2).start()
             fx_copy(kind, 0, d).start()
-            sb_copy(kind, 0, d).start()
+            sib_copy(kind, 0, d, 2).start()
+            keep(kind, d, 2).start()
     gain_finish(1)
     z_step(1, 4)
     ag_b(1)
@@ -458,12 +473,11 @@
         for p in range(2):
             for d in range(2):
                 a_copy(kind, d, p).wait_recv()
-                f[kind][out_unit(kind, 0, d, mine_u[p])] = (
-                    g[kind][unit(kind, y, d, mine_u[p])].astype(F32) + xa[kind, d, p].astype(F32)
-                ).astype(BF16)
+                at = unit(kind, y, d, mine_u[p])
+                xa[kind, d, p] = (g[kind][at].astype(F32) + xa[kind, d, p].astype(F32)).astype(BF16)
                 ag_copy(kind, 0, d, p).start()
-        for d in range(2):
-            sa_copy(kind, 0, d).start()
+                sib_copy(kind, 0, d, p).start()
+                keep(kind, d, p).start()
     ag_b(2)
 
     @pl.loop(1, NY)
@@ -531,6 +545,7 @@
     def all_sent(sem, ref):
         remote(ref, ref, sem, sib_r.at[0], sib).wait_send()
 
+    pltpu.make_async_copy(rr.at[0, pl.ds(0, 2)], rr.at[1, pl.ds(0, 2)], lsem.at[4]).wait()
     all_sent(s_cot, cot.at[pl.ds(0, ROWS - OWN)])
     all_sent(s_ex, gu)
     all_sent(s_rs, rr)
@@ -545,16 +560,31 @@
     all_sent(s_gn, gacc.at[pl.ds(0, GAIN_ROUNDS)])
 
 
+def store(*refs):
+    sem = refs[-1]
+    copies = []
+    for i in range(5):
+        rows = refs[i].shape[0]
+        parts = 4 if rows > OWN else 1
+        for j in range(parts):
+            at = pl.ds(j * (rows // parts), rows // parts)
+            copies.append(pltpu.make_async_copy(refs[i].at[at], refs[5 + i].at[at], sem.at[len(copies)]))
+    for one in copies:
+        one.start()
+    for one in copies:
+        one.wait()
+
+
 def shards(tokens, layer_norm_gain, w_up, w_down, cotangent):
     anywhere = pl.BlockSpec(memory_space=pl.ANY)
     vmem = pl.BlockSpec(memory_space=pltpu.VMEM)
     dma = pltpu.SemaphoreType.DMA
     shapes = [((OWN, D), BF16), ((OWN, D), BF16), ((D, FF), BF16), ((FF, D), BF16), ((1, D), F32)]
-    mixed, grad_tokens, grad_up, grad_down, gain_grad = pl.pallas_call(
+    held = pl.pallas_call(
         kernel,
         out_shape=tuple(pltpu.VMEM(shape, dtype) for shape, dtype in shapes),
         in_specs=[anywhere, vmem, anywhere, anywhere, anywhere],
-        out_specs=(vmem,) * 5,
+        out_specs=(vmem, vmem, anywhere, anywhere, vmem),
         scratch_shapes=[
             pltpu.VMEM((ROWS, D), BF16),
             pltpu.VMEM((D, FF), BF16),
@@ -582,11 +612,11 @@
             pltpu.VMEM((NZ, 1, D), F32),
             pltpu.VMEM((GAIN_ROUNDS + 1, 1, D), F32),
             pltpu.VMEM((GAIN_ROUNDS, 1, D), F32),
-            dma((4,)), dma((12,)),
-            dma((2, 5, 2)), dma((4,)),
-            dma((2, NY - 1, 2, 3)), dma((2, NY, 2)), dma((2, 2, 2)),
-            dma((2, NZ - 1, 2)), dma((2,)),
-            dma((2, NY - 1, 2, 3)), dma((1,)), dma((2, NY, 2)),
+            dma((5,)), dma((12,)),
+            dma((16,)), dma((4,)),
+            dma((90,)), dma((32,)), dma((8,)),
+            dma((30,)), dma((2,)),
+            dma((90,)), dma((1,)), dma((32,)),
             dma((1,)), dma((GAIN_ROUNDS,)),
         ],
         compiler_params=pltpu.CompilerParams(
@@ -597,6 +627,16 @@
         ),
         name="mlp_block",
     )(tokens, layer_norm_gain.reshape(1, D), w_up, w_down, cotangent)
+    mixed, grad_tokens, grad_up, grad_down, gain_grad = pl.pallas_call(
+        store,
+        out_shape=tuple(jax.ShapeDtypeStruct(shape, dtype) for shape, dtype in shapes),
+        in_specs=[vmem] * 5,
+        out_specs=(anywhere,) * 5,
+        scratch_shapes=[dma((11,))],
+        compiler_params=pltpu.CompilerParams(vmem_limit_bytes=2**20),
+        cost_estimate=pl.CostEstimate(flops=0, bytes_accessed=10 * 2**20, transcendentals=0),
+        name="store",
+    )(*(pltpu.with_memory_space_constraint(one, pltpu.VMEM) for one in held))
     return mixed, grad_tokens, grad_up, grad_down, gain_grad.reshape(D)
 
 

time: 134 us -> 126 us (0.940)
  local copies, waits for them, and re-layouts: 6.25 us -> 0 us
  Pallas kernels: 127 us -> 125 us
    unnamed x5 -> x0, local copies, waits for them, and re-layouts: 6.25 us -> none
    pallas_call x1, Pallas kernels: 127 us -> 121 us  [shards(): pl.pallas_call(kernel, out_shape=tuple((pltpu.VMEM(shape, dtype) for shap...]
    pallas_call x0 -> x1, Pallas kernels: none -> 3.8 us  [shards(): pl.pallas_call(store, out_shape=tuple((jax.ShapeDtypeStruct(shape, dtype)...]
where the time goes in v3:
time: 126 us
  Pallas kernels  125 us (99%)
    pallas_call x1, Pallas kernels, shards(): pl.pallas_call(kernel, out_shape=tuple((pltpu.VMEM(shape, dtype) for shap...  121 us
    pallas_call x1, Pallas kernels, shards(): pl.pallas_call(store, out_shape=tuple((jax.ShapeDtypeStruct(shape, dtype)...  3.8 us

profile of v3, /device:TPU:1, one launch (start us, length us, event | category | flops | bytes accessed | tf_op | source)
XLA Modules:
  0.0 125.9 jit_solution(5117160902778589928)
XLA Ops:
  0.6 121.5 %mlp_block.1 = (bf16[16,3072]{1,0:T(8,128)(2,1)S(1)}, bf16[16,3072]{1,0:T(8,128)(2,1)S(1)}, bf16[3072,768]{1,0:T(8,128)(2,1)S(1)}, bf16[768,3072]{1,0:T(8,128)(2,1)S(1)}, f32[1,3072]{1,0:T(1,128)S(1)}) custom-call(bf16[256,3072]{1,0:T(8,128)(2,1)} %tok_hbm.1, f32[1,3072]{1,0:T(1,128)} %bitcast.2, bf16[3072,768]{1,0:T(8,128)(2,1)} %wu_hbm.1, ...), custom_call_target="tpu_custom_call" | custom-call | flops 7247757312 | bytes 23068672 | tf_op jit(solution)/shard_map/mlp_block/pallas_call | solution.py:583
  122.1 3.8 %store.1 = (bf16[16,3072]{1,0:T(8,128)(2,1)}, bf16[16,3072]{1,0:T(8,128)(2,1)}, bf16[3072,768]{1,0:T(8,128)(2,1)}, bf16[768,3072]{1,0:T(8,128)(2,1)}, f32[1,3072]{1,0:T(1,128)}) custom-call(bf16[16,3072]{1,0:T(8,128)(2,1)S(1)} %get-tuple-element.15.refs_0_, bf16[16,3072]{1,0:T(8,128)(2,1)S(1)} %get-tuple-element.16.refs_1_, ...), custom_call_target="tpu_custom_call" | custom-call | bytes 10485760 | tf_op jit(solution)/shard_map/store/pallas_call | solution.py:630

commit v4 on v3

--- a/solution.py
+++ b/solution.py
@@ -17,7 +17,7 @@
 NZ = 8
 OWN = 16
 UC, DC = 192, 96
-UR, UW = 48, 384
+UR, DR, UW = 64, 48, 384
 U, DN = 0, 1
 GAIN_ROUNDS = 6
 
@@ -42,7 +42,7 @@
 
 def flat(*at):
     place = (at[0] * NY + at[1]) * 2 + at[2]
-    return place if len(at) == 3 else place * 3 + at[3]
+    return place if len(at) == 3 else place * 2 + at[3]
 
 
 def mod8(v):
@@ -57,7 +57,7 @@
     tok_hbm, gain, wu_hbm, wd_hbm, cot_hbm,
     mixed, gtok, fu, fd, ggain,
     tok, wu, wd, nrm, mean, inv, nT, nTs, cot, cot_sib, act, slope, aT, bp, brp, bnp,
-    zrecv, zx, gu, gd, rr, xr, xa, gz, gacc, grecv,
+    zrecv, zx, gu, gd, rau, rad, rbu, rbd, xru, xrd, xau, xad, gz, gacc, grecv,
     lsem, sent, crsem, exr, rs_r, xs_r, xa_r, z_r, zx_r, ag_r, sib_r, fx_r, gz_r, gn_r,
 ):
     dp = lax.axis_index("dp")
@@ -68,7 +68,9 @@
     z = lax.rem(mp, NZ)
     xl = mp // NZ
 
-    s_cot, s_ex, s_rs, s_x1, s_xa, s_z, s_zx, s_ag, s_sib, s_fx, s_gz, s_gn = (sent.at[i] for i in range(12))
+    s_cot, s_ex, s_z, s_zx, s_sib, s_gz, s_gn = (sent.at[i] for i in range(7))
+    s_rs, s_ag = (tuple(sent.at[7 + 4 * j + i] for i in range(4)) for j in range(2))
+    s_x1, s_xa, s_fx = (tuple(sent.at[15 + 2 * j + i] for i in range(2)) for j in range(3))
 
     def at_y(v):
         return (xh * 16 + v * 2 + c, mp)
@@ -235,46 +237,59 @@
     def unit(kind, k, d, u, n=1, base=0):
         if kind == U:
             return (pl.ds(pl.multiple_of(base + k * UC + u * UR, 16), n * UR), pl.ds(d * UW, UW))
-        return (pl.ds(pl.multiple_of(k * DC + d * UR, 16), UR), pl.ds(pl.multiple_of(base + u * UW, 128), n * UW))
+        return (pl.ds(pl.multiple_of(k * DC + d * DR, 16), DR), pl.ds(pl.multiple_of(base + u * UW, 128), n * UW))
 
     g = (gu, gd)
     f = (fu, fd)
     kinds = (DN, U)
-    mine_u = (1, 2, 3 * xh)
+    top = (2, 3)
+    ra, rb, xr, xa = (rau, rad), (rbu, rbd), (xru, xrd), (xau, xad)
+
+    def piece(kind, p):
+        return (1, top[kind] - 1) if p == 0 else (top[kind] * xh, 1)
+
+    def other(kind):
+        return top[kind] * (1 - xh)
+
+    def sort(kind, p):
+        return kind + 2 * p
 
     def rs_chunk(s, d):
         return mod8(y - sign[d] * (1 + s))
 
     def x_first(kind, s, d):
         return remote(
-            g[kind].at[unit(kind, rs_chunk(s, d), d, 3 - 3 * xh)], xr.at[kind, s, d],
-            s_x1, xs_r.at[flat(kind, s, d)], xpart,
+            g[kind].at[unit(kind, rs_chunk(s, d), d, other(kind))], xr[kind].at[s, d],
+            s_x1[kind], xs_r.at[flat(kind, s, d)], xpart,
         )
 
     def x_first_start(kind, s):
         for d in range(2):
             x_first(kind, s, d).start()
+
+    def rs_slot(kind, s, d, p):
+        return (ra, rb)[p][kind].at[s, d]
 
     def rs_copy(kind, s, d, p):
         return remote(
-            g[kind].at[unit(kind, rs_chunk(s, d), d, mine_u[p])], rr.at[kind, s, d, p],
-            s_rs, rs_r.at[flat(kind, s, d, p)], ydev[d],
+            g[kind].at[unit(kind, rs_chunk(s, d), d, *piece(kind, p))], rs_slot(kind, s, d, p),
+            s_rs[sort(kind, p)], rs_r.at[flat(kind, s, d, p)], ydev[d],
         )
 
-    def rs_step(kind, s, pieces=(0, 1, 2), first=False, last=False):
-        for p in pieces:
+    def rs_step(kind, s, which=(0, 1), first=False, last=False):
+        for p in which:
             for d in range(2):
-                at = unit(kind, rs_chunk(s, d), d, mine_u[p])
-                if p == 2:
+                at = unit(kind, rs_chunk(s, d), d, *piece(kind, p))
+                if p == 1:
                     x_first(kind, s, d).wait_recv()
                 if not first:
                     rs_copy(kind, s - 1, d, p).wait_recv()
-                if p == 2 or not first:
+                if p == 1 or not first:
                     total = g[kind][at].astype(F32)
-                    if p == 2:
-                        total = total + xr[kind, s, d].astype(F32)
+                    if p == 1:
+                        total = total + xr[kind][s, d].astype(F32)
                     if not first:
-                        total = total + rr[kind, s - 1, d, p].astype(F32)
+                        total = total + rs_slot(kind, s - 1, d, p)[...].astype(F32)
                     g[kind][at] = total.astype(BF16)
                 if not last:
                     rs_copy(kind, s, d, p).start()
@@ -291,7 +306,7 @@
         ).astype(BF16)
 
     x_first_start(DN, 0)
-    rs_step(DN, 0, (0, 1), first=True)
+    rs_step(DN, 0, (0,), first=True)
     x_first_start(DN, 1)
 
     remote(nTs, nT.at[:, theirsK], s_ex, exr.at[1], sib).wait_recv()
@@ -303,7 +318,7 @@
         gu[rows, :] = dot_nn(nT[rows, :], bp[...]).astype(BF16)
 
     x_first_start(U, 0)
-    rs_step(U, 0, (0, 1), first=True)
+    rs_step(U, 0, (0,), first=True)
     x_first_start(U, 1)
     z_step(0, 1)
 
@@ -331,7 +346,7 @@
         if r + 1 < GAIN_ROUNDS:
             gain_copy(r + 1).start()
 
-    rs_step(DN, 0, (2,), first=True)
+    rs_step(DN, 0, (1,), first=True)
     x_first_start(DN, 2)
 
     @pl.loop(0, D // 512)
@@ -342,7 +357,7 @@
         hat = (tok[:, cols].astype(F32) - mean[...]) * inv[...]
         gz[z, :, cols] = jnp.sum(back * hat, axis=0, keepdims=True)
 
-    rs_step(U, 0, (2,), first=True)
+    rs_step(U, 0, (1,), first=True)
     x_first_start(U, 2)
     z_step(0, 2)
     for j in range(1, NZ):
@@ -382,9 +397,9 @@
         def _():
             gain_finish(0)
 
-    def a_copy(kind, d, p):
+    def a_copy(kind, d):
         return remote(
-            g[kind].at[unit(kind, y, d, mine_u[p])], xa.at[kind, d, p], s_xa, xa_r.at[kind * 4 + d * 2 + p], xpart,
+            g[kind].at[unit(kind, y, d, *piece(kind, 0))], xa[kind].at[d], s_xa[kind], xa_r.at[kind * 2 + d], xpart,
         )
 
     def ag_chunk(s, d):
@@ -394,91 +409,86 @@
         return unit(kind, ag_chunk(s, d), d, u, n, c * HALF)
 
     def own(kind, d, p):
-        return xa.at[kind, d, p] if p < 2 else g[kind].at[unit(kind, y, d, 3 * xh)]
+        return xa[kind].at[d] if p == 0 else g[kind].at[unit(kind, y, d, *piece(kind, 1))]
 
     def out_copy(kind, s, d, p, ssem, rsem, to):
-        dst = f[kind].at[out_unit(kind, s, d, mine_u[p])]
+        dst = f[kind].at[out_unit(kind, s, d, *piece(kind, p))]
         return remote(own(kind, d, p) if isinstance(s, int) and s == 0 else dst, dst, ssem, rsem, to)
 
     def ag_copy(kind, s, d, p):
-        return out_copy(kind, s, d, p, s_ag, ag_r.at[flat(kind, s, d, p)], ydev[d])
+        return out_copy(kind, s, d, p, s_ag[sort(kind, p)], ag_r.at[flat(kind, s, d, p)], ydev[d])
 
     def ag_arrival(kind, s, d, p):
-        at = f[kind].at[out_unit(kind, s, d, mine_u[p])]
-        return remote(at, at, s_ag, ag_r.at[flat(kind, s - 1, d, p)], ydev[d])
-
-    def sib_copy(kind, s, d, p):
-        return out_copy(kind, s, d, p, s_sib, sib_r.at[0], sib)
-
-    def sa_copy(kind, s, d):
-        at = f[kind].at[out_unit(kind, s, d, 1, 2)]
-        return remote(at, at, s_sib, sib_r.at[0], sib)
+        at = f[kind].at[out_unit(kind, s, d, *piece(kind, p))]
+        return remote(at, at, s_ag[sort(kind, p)], ag_r.at[flat(kind, s - 1, d, p)], ydev[d])
+
+    def own_to_sib(kind, d, p):
+        return out_copy(kind, 0, d, p, s_sib, sib_r.at[0], sib)
 
     def fx_copy(kind, s, d):
-        return out_copy(kind, s, d, 2, s_fx, fx_r.at[flat(kind, s, d)], xpart)
+        return out_copy(kind, s, d, 1, s_fx[kind], fx_r.at[flat(kind, s, d)], xpart)
 
     def keep(kind, d, p):
-        return pltpu.make_async_copy(own(kind, d, p), f[kind].at[out_unit(kind, 0, d, mine_u[p])], lsem.at[4])
+        dst = f[kind].at[out_unit(kind, 0, d, *piece(kind, p))]
+        return pltpu.make_async_copy(own(kind, d, p), dst, lsem.at[4 + sort(kind, p)])
 
     def fx_arrival(kind, s, d):
-        at = f[kind].at[out_unit(kind, s, d, 3 - 3 * xh)]
-        return remote(at, at, s_fx, fx_r.at[flat(kind, s, d)], xpart)
-
-    def sx_copy(kind, s, d):
-        at = f[kind].at[out_unit(kind, s, d, 3 - 3 * xh)]
+        at = f[kind].at[out_unit(kind, s, d, other(kind))]
+        return remote(at, at, s_fx[kind], fx_r.at[flat(kind, s, d)], xpart)
+
+    def to_sib(kind, s, d, u, n):
+        at = f[kind].at[out_unit(kind, s, d, u, n)]
         return remote(at, at, s_sib, sib_r.at[0], sib)
 
     def x_arrived(s):
         for kind in kinds:
             for d in range(2):
                 fx_arrival(kind, s, d).wait_recv()
-                sx_copy(kind, s, d).start()
+                if isinstance(s, int) and s == 0:
+                    to_sib(kind, s, d, other(kind), 1).start()
+                else:
+                    to_sib(kind, s, d, 0, top[kind] + 1).start()
 
     def ag_a(s, send=True):
         for kind in kinds:
-            for p in range(2):
-                for d in range(2):
-                    ag_arrival(kind, s, d, p).wait_recv()
-                    if send:
-                        ag_copy(kind, s, d, p).start()
-        for kind in kinds:
             for d in range(2):
-                sa_copy(kind, s, d).start()
+                ag_arrival(kind, s, d, 0).wait_recv()
+                if send:
+                    ag_copy(kind, s, d, 0).start()
 
     def ag_b(s, send=True):
         for kind in kinds:
             for d in range(2):
-                ag_arrival(kind, s, d, 2).wait_recv()
+                ag_arrival(kind, s, d, 1).wait_recv()
                 if send:
-                    ag_copy(kind, s, d, 2).start()
+                    ag_copy(kind, s, d, 1).start()
                 fx_copy(kind, s, d).start()
-        for kind in kinds:
-            for d in range(2):
-                sib_copy(kind, s, d, 2).start()
 
     for kind in kinds:
         rs_step(kind, 7, last=True)
-        for p in range(2):
-            for d in range(2):
-                a_copy(kind, d, p).start()
-        for d in range(2):
-            ag_copy(kind, 0, d, 2).start()
+        for d in range(2):
+            a_copy(kind, d).start()
+        for d in range(2):
+            ag_copy(kind, 0, d, 1).start()
             fx_copy(kind, 0, d).start()
-            sib_copy(kind, 0, d, 2).start()
-            keep(kind, d, 2).start()
+    for kind in kinds:
+        for d in range(2):
+            own_to_sib(kind, d, 1).start()
+            keep(kind, d, 1).start()
     gain_finish(1)
     z_step(1, 4)
     ag_b(1)
     for kind in kinds:
-        for p in range(2):
-            for d in range(2):
-                a_copy(kind, d, p).wait_recv()
-                at = unit(kind, y, d, mine_u[p])
-                xa[kind, d, p] = (g[kind][at].astype(F32) + xa[kind, d, p].astype(F32)).astype(BF16)
-                ag_copy(kind, 0, d, p).start()
-                sib_copy(kind, 0, d, p).start()
-                keep(kind, d, p).start()
+        for d in range(2):
+            a_copy(kind, d).wait_recv()
+            xa[kind][d] = (g[kind][unit(kind, y, d, *piece(kind, 0))].astype(F32) + xa[kind][d].astype(F32)).astype(BF16)
+            ag_copy(kind, 0, d, 0).start()
     ag_b(2)
+    for kind in kinds:
+        for d in range(2):
+            own_to_sib(kind, d, 0).start()
+            keep(kind, d, 0).start()
+    x_arrived(0)
 
     @pl.loop(1, NY)
     def _(s):
@@ -498,7 +508,9 @@
         def _():
             ag_b(7, False)
 
-        x_arrived(s - 1)
+        @pl.when(s > 1)
+        def _():
+            x_arrived(s - 1)
 
         @pl.when(s < 3)
         def _():
@@ -545,17 +557,20 @@
     def all_sent(sem, ref):
         remote(ref, ref, sem, sib_r.at[0], sib).wait_send()
 
-    pltpu.make_async_copy(rr.at[0, pl.ds(0, 2)], rr.at[1, pl.ds(0, 2)], lsem.at[4]).wait()
+    for i, ref in enumerate((xau, xad, xru.at[0], xrd.at[0])):
+        pltpu.make_async_copy(ref, ref, lsem.at[4 + i]).wait()
     all_sent(s_cot, cot.at[pl.ds(0, ROWS - OWN)])
     all_sent(s_ex, gu)
-    all_sent(s_rs, rr)
-    all_sent(s_x1, xr)
-    all_sent(s_xa, xa)
+    for i, ref in enumerate((rau, rad, rbu, rbd)):
+        all_sent(s_rs[i], ref)
+        all_sent(s_ag[i], ref)
+    for kind in kinds:
+        all_sent(s_xa[kind], xa[kind])
+        all_sent(s_x1[kind], xr[kind])
+        all_sent(s_fx[kind], xr[kind])
     all_sent(s_z, zrecv)
     all_sent(s_zx, zx)
-    all_sent(s_ag, rr)
     all_sent(s_sib, fu)
-    all_sent(s_fx, xr)
     all_sent(s_gz, gz.at[pl.ds(0, NZ - 1)])
     all_sent(s_gn, gacc.at[pl.ds(0, GAIN_ROUNDS)])
 
@@ -606,17 +621,22 @@
             pltpu.VMEM((2, OWN, D), BF16),
             pltpu.VMEM((HALF, FF), BF16),
             pltpu.VMEM((FF, HALF), BF16),
-            pltpu.VMEM((2, NY - 1, 2, 3, UR, UW), BF16),
-            pltpu.VMEM((2, NY, 2, UR, UW), BF16),
-            pltpu.VMEM((2, 2, 2, UR, UW), BF16),
+            pltpu.VMEM((NY - 1, 2, UR, UW), BF16),
+            pltpu.VMEM((NY - 1, 2, DR, 2 * UW), BF16),
+            pltpu.VMEM((NY - 1, 2, UR, UW), BF16),
+            pltpu.VMEM((NY - 1, 2, DR, UW), BF16),
+            pltpu.VMEM((NY, 2, UR, UW), BF16),
+            pltpu.VMEM((NY, 2, DR, UW), BF16),
+            pltpu.VMEM((2, UR, UW), BF16),
+            pltpu.VMEM((2, DR, 2 * UW), BF16),
             pltpu.VMEM((NZ, 1, D), F32),
             pltpu.VMEM((GAIN_ROUNDS + 1, 1, D), F32),
             pltpu.VMEM((GAIN_ROUNDS, 1, D), F32),
-            dma((5,)), dma((12,)),
+            dma((8,)), dma((21,)),
             dma((16,)), dma((4,)),
-            dma((90,)), dma((32,)), dma((8,)),
+            dma((60,)), dma((32,)), dma((4,)),
             dma((30,)), dma((2,)),
-            dma((90,)), dma((1,)), dma((32,)),
+            dma((60,)), dma((1,)), dma((32,)),
             dma((1,)), dma((GAIN_ROUNDS,)),
         ],
         compiler_params=pltpu.CompilerParams(

time: 126 us -> 125 us (level)
  no operation moved by 1% of the time
where the time goes in v4:
time: 125 us
  Pallas kernels  124 us (99%)
    pallas_call x1, Pallas kernels, shards(): pl.pallas_call(kernel, out_shape=tuple((pltpu.VMEM(shape, dtype) for shap...  121 us
    pallas_call x1, Pallas kernels, shards(): pl.pallas_call(store, out_shape=tuple((jax.ShapeDtypeStruct(shape, dtype)...  3.8 us

profile of v4, /device:TPU:1, one launch (start us, length us, event | category | flops | bytes accessed | tf_op | source)
XLA Modules:
  0.0 125.1 jit_solution(14316428588273644440)
XLA Ops:
  0.6 120.7 %mlp_block.1 = (bf16[16,3072]{1,0:T(8,128)(2,1)S(1)}, bf16[16,3072]{1,0:T(8,128)(2,1)S(1)}, bf16[3072,768]{1,0:T(8,128)(2,1)S(1)}, bf16[768,3072]{1,0:T(8,128)(2,1)S(1)}, f32[1,3072]{1,0:T(1,128)S(1)}) custom-call(bf16[256,3072]{1,0:T(8,128)(2,1)} %tok_hbm.1, f32[1,3072]{1,0:T(1,128)} %bitcast.2, bf16[3072,768]{1,0:T(8,128)(2,1)} %wu_hbm.1, ...), custom_call_target="tpu_custom_call" | custom-call | flops 7247757312 | bytes 23068672 | tf_op jit(solution)/shard_map/mlp_block/pallas_call | solution.py:598
  121.3 3.8 %store.1 = (bf16[16,3072]{1,0:T(8,128)(2,1)}, bf16[16,3072]{1,0:T(8,128)(2,1)}, bf16[3072,768]{1,0:T(8,128)(2,1)}, bf16[768,3072]{1,0:T(8,128)(2,1)}, f32[1,3072]{1,0:T(1,128)}) custom-call(bf16[16,3072]{1,0:T(8,128)(2,1)S(1)} %get-tuple-element.15.refs_0_, bf16[16,3072]{1,0:T(8,128)(2,1)S(1)} %get-tuple-element.16.refs_1_, ...), custom_call_target="tpu_custom_call" | custom-call | bytes 10485760 | tf_op jit(solution)/shard_map/store/pallas_call | solution.py:650
